TPU v7x, 1024 devices: a whole 4x4x32 slice. The times are simulated.
1024 devices in a mesh: expert: 32 (over z), dp: 32 (over y, x, core).
Axes of the slice: x: 4, y: 4, z: 32, core: 2. Of those that a mesh axis runs over, the one named last changes fastest.
Arguments:
- rows_in: bfloat16 [16384, 4096], P('expert', 'dp'), may hold values from -6 to 6
- out_grad: bfloat16 [16384, 4096], P('expert', 'dp'), may hold values from -6 to 6
- route_weight: float32 [16384], P('expert'), may hold values from 0.1 to 1
- live_rows: int32 [32], P('expert'), may hold values from 1 to 512, as said below
- expert_of_group: int32 [32], replicated, may hold values from 0 to 31, as said below
- gate_weight: bfloat16 [32, 1536, 4096], P(None, 'expert', 'dp'), may hold values from -0.09375 to 0.09375
- up_weight: bfloat16 [32, 1536, 4096], P(None, 'expert', 'dp'), may hold values from -0.09375 to 0.09375
- down_weight: bfloat16 [32, 1536, 4096], P(None, 'expert', 'dp'), may hold values from -0.15625 to 0.15625
Outputs:
- rows_grad: bfloat16 [16384, 4096], P('expert', 'dp')
- gate_grad: bfloat16 [32, 1536, 4096], P(None, 'expert', 'dp')
- up_grad: bfloat16 [32, 1536, 4096], P(None, 'expert', 'dp')
- down_grad: bfloat16 [32, 1536, 4096], P(None, 'expert', 'dp')
Inputs may be any that keep to these rules, and one draw needn't show every extreme that they name: `live_rows`: rows at or past a group's count are padding; some group has all 512 slots live. `expert_of_group`: several groups may use the same expert.
All inputs are finite; a program needn't handle non-finite values.
Results may differ from a plain program's by a relative error of at most 0.03.
Values may be sent and summed in bfloat16 or wider, within the bound.
No kernel may reach another device: no remote copies, remote signals or barrier semaphores. Data moves between devices by JAX's collectives and lax.ppermute only.
A program may use at most 32 MiB of HBM per device.

v0:
```python
import jax
import jax.numpy as jnp
from jax import lax
from jax.sharding import PartitionSpec as P


def width_product(left_rows, right_rows):
    summed = jnp.einsum("rd,fd->rf", left_rows, right_rows, preferred_element_type=jnp.float32)
    return summed.astype(jnp.bfloat16).astype(jnp.float32)


def shards(
    rows_in, out_grad, route_weight, live_rows, expert_of_group, gate_weight, up_weight, down_weight
):
    groups = lax.axis_size("expert")
    experts_all = gate_weight.shape[0]
    unit_piece = gate_weight.shape[1]
    piece_width = gate_weight.shape[2]
    units_all = unit_piece * groups
    row_count = rows_in.shape[0]
    outgoing = (
        gate_weight[expert_of_group],
        up_weight[expert_of_group],
        down_weight[expert_of_group],
    )
    fetched = (
        lax.all_to_all(outgoing[0], "expert", split_axis=0, concat_axis=0, tiled=True),
        lax.all_to_all(outgoing[1], "expert", split_axis=0, concat_axis=0, tiled=True),
        lax.all_to_all(outgoing[2], "expert", split_axis=0, concat_axis=0, tiled=True),
    )
    w_gate = fetched[0].reshape(units_all, piece_width)
    w_up = fetched[1].reshape(units_all, piece_width)
    w_down = fetched[2].reshape(units_all, piece_width)
    position = jnp.arange(row_count, dtype=jnp.int32)
    live_mask = (position < live_rows[0]).astype(jnp.float32)
    scaled = (out_grad.astype(jnp.float32) * (route_weight * live_mask)[:, None]).astype(
        jnp.bfloat16
    )
    partials = (
        width_product(rows_in, w_gate),
        width_product(rows_in, w_up),
        width_product(scaled, w_down),
    )
    gate_sum, up_sum, hidden_grad = (
        lax.psum_scatter(
            partials[0].astype(jnp.bfloat16), "dp", scatter_dimension=1, tiled=True
        ).astype(jnp.float32),
        lax.psum_scatter(
            partials[1].astype(jnp.bfloat16), "dp", scatter_dimension=1, tiled=True
        ).astype(jnp.float32),
        lax.psum_scatter(
            partials[2].astype(jnp.bfloat16), "dp", scatter_dimension=1, tiled=True
        ).astype(jnp.float32),
    )
    sigmoid_gate = jax.nn.sigmoid(gate_sum)
    activated = gate_sum * sigmoid_gate
    hidden_act = (activated * up_sum).astype(jnp.bfloat16)
    up_rows_grad = (hidden_grad * activated).astype(jnp.bfloat16)
    gate_rows_grad = (
        hidden_grad * up_sum * sigmoid_gate * (1.0 + gate_sum * (1.0 - sigmoid_gate))
    ).astype(jnp.bfloat16)
    hidden_act, gate_rows_grad, up_rows_grad = (
        lax.all_gather(hidden_act, "dp", axis=1, tiled=True),
        lax.all_gather(gate_rows_grad, "dp", axis=1, tiled=True),
        lax.all_gather(up_rows_grad, "dp", axis=1, tiled=True),
    )
    rows_grad = (
        jnp.dot(gate_rows_grad, w_gate, preferred_element_type=jnp.float32)
        + jnp.dot(up_rows_grad, w_up, preferred_element_type=jnp.float32)
    ).astype(jnp.bfloat16)
    term_gate = jnp.einsum(
        "rf,rd->fd", gate_rows_grad, rows_in, preferred_element_type=jnp.float32
    ).astype(jnp.bfloat16)
    term_up = jnp.einsum(
        "rf,rd->fd", up_rows_grad, rows_in, preferred_element_type=jnp.float32
    ).astype(jnp.bfloat16)
    term_down = jnp.einsum(
        "rf,rd->fd", hidden_act, scaled, preferred_element_type=jnp.float32
    ).astype(jnp.bfloat16)
    returned = (
        lax.all_to_all(
            term_gate.reshape(groups, unit_piece, piece_width),
            "expert",
            split_axis=0,
            concat_axis=0,
            tiled=True,
        ),
        lax.all_to_all(
            term_up.reshape(groups, unit_piece, piece_width),
            "expert",
            split_axis=0,
            concat_axis=0,
            tiled=True,
        ),
        lax.all_to_all(
            term_down.reshape(groups, unit_piece, piece_width),
            "expert",
            split_axis=0,
            concat_axis=0,
            tiled=True,
        ),
    )
    owner_table = (
        expert_of_group[:, None] == jnp.arange(experts_all, dtype=jnp.int32)[None, :]
    ).astype(jnp.bfloat16)
    gate_grad = jnp.einsum(
        "ge,gfd->efd", owner_table, returned[0], preferred_element_type=jnp.float32
    ).astype(jnp.bfloat16)
    up_grad = jnp.einsum(
        "ge,gfd->efd", owner_table, returned[1], preferred_element_type=jnp.float32
    ).astype(jnp.bfloat16)
    down_grad = jnp.einsum(
        "ge,gfd->efd", owner_table, returned[2], preferred_element_type=jnp.float32
    ).astype(jnp.bfloat16)
    return (rows_grad, gate_grad, up_grad, down_grad)


def solution(mesh):
    return jax.shard_map(
        shards,
        mesh=mesh,
        in_specs=(
            P("expert", "dp"),
            P("expert", "dp"),
            P("expert"),
            P("expert"),
            P(),
            P(None, "expert", "dp"),
            P(None, "expert", "dp"),
            P(None, "expert", "dp"),
        ),
        out_specs=(
            P("expert", "dp"),
            P(None, "expert", "dp"),
            P(None, "expert", "dp"),
            P(None, "expert", "dp"),
        ),
        check_vma=False,
    )
```

profile of v0, /device:TPU:1, one launch (start us, length us, event | category | flops | bytes accessed | tf_op | source)
XLA Modules:
  0.0 848.5 jit_solution(18165989317400670592)
XLA Ops:
  9.5 29.3 %all-to-all-start = ((bf16[32,48,128]{2,1,0:T(8,128)(2,1)}), bf16[32,48,128]{2,1,0:T(8,128)(2,1)S(1)}, u32[]{:S(2)}, u32[]{:S(2)}) async-start(bf16[32,48,128]{2,1,0:T(8,128)(2,1)} %gather_fusion), calls=%async_computation | async-start | bytes 786432 | tf_op jit(solution)/shard_map/all_to_all | solution.py:29
  38.8 1.3 gather_fusion.1
  40.2 50.6 %all-to-all-done = bf16[32,48,128]{2,1,0:T(8,128)(2,1)S(1)} async-done(((bf16[32,48,128]{2,1,0:T(8,128)(2,1)}), bf16[32,48,128]{2,1,0:T(8,128)(2,1)S(1)}, u32[]{:S(2)}, u32[]{:S(2)}) %all-to-all-start) | async-done | bytes 393248 | tf_op jit(solution)/shard_map/all_to_all | solution.py:29
  90.8 4.4 all-to-all-start.1
  95.9 1.9 convolution_convert_fusion.2
  99.1 45.1 %all-to-all-done.1 = bf16[32,48,128]{2,1,0:T(8,128)(2,1)S(1)} async-done(((bf16[32,48,128]{2,1,0:T(8,128)(2,1)}), bf16[32,48,128]{2,1,0:T(8,128)(2,1)S(1)}, u32[]{:S(2)}, u32[]{:S(2)}) %all-to-all-start.1) | async-done | bytes 393248 | tf_op jit(solution)/shard_map/all_to_all | solution.py:28
  144.3 6.8 all-to-all-start.2
  151.1 1.7 fusion
  152.9 44.3 %all-to-all-done.2 = bf16[32,48,128]{2,1,0:T(8,128)(2,1)S(1)} async-done(((bf16[32,48,128]{2,1,0:T(8,128)(2,1)}), bf16[32,48,128]{2,1,0:T(8,128)(2,1)S(1)}, u32[]{:S(2)}, u32[]{:S(2)}) %all-to-all-start.2) | async-done | bytes 393248 | tf_op jit(solution)/shard_map/all_to_all | solution.py:27
  197.2 1.8 fusion.1
  199.0 35.2 %reduce-scatter.4.cloned.1.call-done = bf16[512,48]{0,1:T(8,128)(2,1)} async-done(((bf16[512,1536]{0,1:T(8,128)(2,1)}), bf16[512,48]{0,1:T(8,128)(2,1)}) %reduce-scatter.4.cloned.1.call-update) | async-done | bytes 49168 | tf_op jit(solution)/shard_map/reduce_scatter | solution.py:51
  234.2 137.4 %reduce-scatter.6.cloned.1.call-done = bf16[512,48]{0,1:T(8,128)(2,1)} async-done(((bf16[512,1536]{0,1:T(8,128)(2,1)}), bf16[512,48]{0,1:T(8,128)(2,1)}) %reduce-scatter.6.cloned.1.call-update) | async-done | bytes 49168 | tf_op jit(solution)/shard_map/reduce_scatter | solution.py:48
  371.6 137.4 %reduce-scatter.8.cloned.1.call-done = bf16[512,48]{0,1:T(8,128)(2,1)} async-done(((bf16[512,1536]{0,1:T(8,128)(2,1)}), bf16[512,48]{0,1:T(8,128)(2,1)}) %reduce-scatter.8.cloned.1.call-update) | async-done | bytes 49168 | tf_op jit(solution)/shard_map/reduce_scatter | solution.py:45
  508.9 1.6 fusion.10
  511.1 83.4 %all-gather.6.cloned.1.call-done = bf16[512,1536]{0,1:T(8,128)(2,1)} async-done(((bf16[512,48]{0,1:T(8,128)(2,1)}), bf16[512,1536]{0,1:T(8,128)(2,1)}) %all-gather.6.cloned.1.call-update) | async-done | bytes 1572880 | tf_op jit(solution)/shard_map/all_gather | solution.py:65
  594.5 2.7 convolution_convert_fusion.4
  597.2 22.6 %all-to-all-start.4 = ((bf16[32,48,128]{2,1,0:T(8,128)(2,1)}), bf16[32,48,128]{2,1,0:T(8,128)(2,1)S(1)}, u32[]{:S(2)}, u32[]{:S(2)}) async-start(bf16[32,48,128]{2,1,0:T(8,128)(2,1)} %bitcast.8), calls=%async_computation.7 | async-start | bytes 786432 | tf_op jit(solution)/shard_map/all_to_all | solution.py:88
  620.4 57.5 %all-gather.4.cloned.1.call-done = bf16[512,1536]{0,1:T(8,128)(2,1)} async-done(((bf16[512,48]{0,1:T(8,128)(2,1)}), bf16[512,1536]{0,1:T(8,128)(2,1)}) %all-gather.4.cloned.1.call-update) | async-done | bytes 1572880 | tf_op jit(solution)/shard_map/all_gather | solution.py:64
  677.9 2.7 convolution_convert_fusion.5
  680.6 22.8 %all-to-all-start.3 = ((bf16[32,48,128]{2,1,0:T(8,128)(2,1)}), bf16[32,48,128]{2,1,0:T(8,128)(2,1)}, u32[]{:S(2)}, u32[]{:S(2)}) async-start(bf16[32,48,128]{2,1,0:T(8,128)(2,1)} %bitcast.7), calls=%async_computation.6 | async-start | bytes 786432 | tf_op jit(solution)/shard_map/all_to_all | solution.py:81
  703.4 57.9 %all-gather.8.cloned.1.call-done = bf16[512,1536]{0,1:T(8,128)(2,1)} async-done(((bf16[512,48]{0,1:T(8,128)(2,1)}), bf16[512,1536]{0,1:T(8,128)(2,1)}) %all-gather.8.cloned.1.call-update) | async-done | bytes 1572880 | tf_op jit(solution)/shard_map/all_gather | solution.py:63
  761.3 2.8 convolution_convert_fusion.3
  764.2 22.8 %all-to-all-start.5 = ((bf16[32,48,128]{2,1,0:T(8,128)(2,1)}), bf16[32,48,128]{2,1,0:T(8,128)(2,1)}, u32[]{:S(2)}, u32[]{:S(2)}) async-start(bf16[32,48,128]{2,1,0:T(8,128)(2,1)} %bitcast.9), calls=%async_computation.8 | async-start | bytes 786432 | tf_op jit(solution)/shard_map/all_to_all | solution.py:95
  793.0 46.6 %all-to-all-done.5 = bf16[32,48,128]{2,1,0:T(8,128)(2,1)} async-done(((bf16[32,48,128]{2,1,0:T(8,128)(2,1)}), bf16[32,48,128]{2,1,0:T(8,128)(2,1)}, u32[]{:S(2)}, u32[]{:S(2)}) %all-to-all-start.5) | async-done | bytes 393248 | tf_op jit(solution)/shard_map/all_to_all | solution.py:95
  (45 shorter events, 13.2 us)
Async XLA Ops:
  7.2 1.0 copy-start
  7.2 31.6 %copy-start.5 = (bf16[32,48,128]{2,1,0:T(8,128)(2,1)S(1)}, bf16[32,48,128]{2,1,0:T(8,128)(2,1)}, u32[]{:S(2)}) copy-start(bf16[32,48,128]{2,1,0:T(8,128)(2,1)} %param.14) | copy-start | bytes 1179652
  8.2 87.7 %copy-start.8 = (f32[512]{0:T(512)S(1)}, f32[512]{0:T(512)}, u32[]{:S(2)}) copy-start(f32[512]{0:T(512)} %param.10) | copy-start | bytes 6148
  8.2 87.7 %copy-start.4 = (bf16[512,128]{1,0:T(8,128)(2,1)S(1)}, bf16[512,128]{1,0:T(8,128)(2,1)}, u32[]{:S(2)}) copy-start(bf16[512,128]{1,0:T(8,128)(2,1)} %param.9) | copy-start | bytes 393220
  9.5 81.2 %all-to-all-start = ((bf16[32,48,128]{2,1,0:T(8,128)(2,1)}), bf16[32,48,128]{2,1,0:T(8,128)(2,1)S(1)}, u32[]{:S(2)}, u32[]{:S(2)}) async-start(bf16[32,48,128]{2,1,0:T(8,128)(2,1)} %gather_fusion), calls=%async_computation | async-start | bytes 786432 | tf_op jit(solution)/shard_map/all_to_all | solution.py:29
  90.8 53.5 %all-to-all-start.1 = ((bf16[32,48,128]{2,1,0:T(8,128)(2,1)}), bf16[32,48,128]{2,1,0:T(8,128)(2,1)S(1)}, u32[]{:S(2)}, u32[]{:S(2)}) async-start(bf16[32,48,128]{2,1,0:T(8,128)(2,1)} %gather_fusion.1), calls=%async_computation.2 | async-start | bytes 786432 | tf_op jit(solution)/shard_map/all_to_all | solution.py:28
  95.2 139.0 %reduce-scatter.4.cloned.1.call-start = ((), (), s32[]{:S(2)}) async-start(), calls=%async_computation.9 | async-start | bytes 1622016 | tf_op jit(solution)/shard_map/reduce_scatter | solution.py:51
  95.9 1.9 copy-start.6
  97.8 53.4 %copy-start.3 = (bf16[512,128]{1,0:T(8,128)(2,1)S(1)}, bf16[512,128]{1,0:T(8,128)(2,1)}, u32[]{:S(2)}) copy-start(bf16[512,128]{1,0:T(8,128)(2,1)} %param.8) | copy-start | bytes 393220
  144.3 52.9 %all-to-all-start.2 = ((bf16[32,48,128]{2,1,0:T(8,128)(2,1)}), bf16[32,48,128]{2,1,0:T(8,128)(2,1)S(1)}, u32[]{:S(2)}, u32[]{:S(2)}) async-start(bf16[32,48,128]{2,1,0:T(8,128)(2,1)} %gather_fusion.2), calls=%async_computation.4 | async-start | bytes 786432 | tf_op jit(solution)/shard_map/all_to_all | solution.py:27
  151.1 220.5 %reduce-scatter.6.cloned.1.call-start = ((), (), s32[]{:S(2)}) async-start(), calls=%async_computation.10 | async-start | bytes 1622016 | tf_op jit(solution)/shard_map/reduce_scatter | solution.py:48
  152.9 356.0 %reduce-scatter.8.cloned.1.call-start = ((), (), s32[]{:S(2)}) async-start(), calls=%async_computation.11 | async-start | bytes 1622016 | tf_op jit(solution)/shard_map/reduce_scatter | solution.py:45
  199.0 395.5 %all-gather.6.cloned.1.call-start = ((), (), s32[]{:S(2)}) async-start(), calls=%async_computation.13 | async-start | bytes 1622016 | tf_op jit(solution)/shard_map/all_gather | solution.py:65
  510.5 167.4 %all-gather.4.cloned.1.call-start = ((), (), s32[]{:S(2)}) async-start(), calls=%async_computation.12 | async-start | bytes 1622016 | tf_op jit(solution)/shard_map/all_gather | solution.py:64
  597.2 83.4 %all-to-all-start.4 = ((bf16[32,48,128]{2,1,0:T(8,128)(2,1)}), bf16[32,48,128]{2,1,0:T(8,128)(2,1)S(1)}, u32[]{:S(2)}, u32[]{:S(2)}) async-start(bf16[32,48,128]{2,1,0:T(8,128)(2,1)} %bitcast.8), calls=%async_computation.7 | async-start | bytes 786432 | tf_op jit(solution)/shard_map/all_to_all | solution.py:88
  619.9 141.5 %all-gather.8.cloned.1.call-start = ((), (), s32[]{:S(2)}) async-start(), calls=%async_computation.14 | async-start | bytes 1622016 | tf_op jit(solution)/shard_map/all_gather | solution.py:63
  680.6 83.6 %all-to-all-start.3 = ((bf16[32,48,128]{2,1,0:T(8,128)(2,1)}), bf16[32,48,128]{2,1,0:T(8,128)(2,1)}, u32[]{:S(2)}, u32[]{:S(2)}) async-start(bf16[32,48,128]{2,1,0:T(8,128)(2,1)} %bitcast.7), calls=%async_computation.6 | async-start | bytes 786432 | tf_op jit(solution)/shard_map/all_to_all | solution.py:81
  703.4 83.6 %copy-start.2 = (bf16[512,1536]{0,1:T(8,128)(2,1)S(1)}, bf16[512,1536]{0,1:T(8,128)(2,1)}, u32[]{:S(2)}) copy-start(bf16[512,1536]{0,1:T(8,128)(2,1)} %all-gather.4.cloned.1.call-done) | copy-start | bytes 4718596
  764.2 75.3 %all-to-all-start.5 = ((bf16[32,48,128]{2,1,0:T(8,128)(2,1)}), bf16[32,48,128]{2,1,0:T(8,128)(2,1)}, u32[]{:S(2)}, u32[]{:S(2)}) async-start(bf16[32,48,128]{2,1,0:T(8,128)(2,1)} %bitcast.9), calls=%async_computation.8 | async-start | bytes 786432 | tf_op jit(solution)/shard_map/all_to_all | solution.py:95
  787.0 1.4 copy-start.1
  788.4 1.3 copy-start.7
Sparse Core Ops, SparseCore 0:
  101.6 132.5 reduce-scatter.3
  239.8 131.7 reduce-scatter.5
  377.1 131.7 reduce-scatter.7
  513.6 80.7 all-gather.5
  599.2 78.6 all-gather.3
  682.6 78.6 all-gather.7
where the time goes:
time: 850 us; the launch traced here: 849 us
  waiting for transfers between devices  696 us (82%)
  starting transfers between devices  109 us (13%)
  matrix products  18.2 us (2%)
  between operations  14.9 us (2%)
    reduce_scatter x1, waiting for transfers between devices, shards(): lax.psum_scatter(partials[0].astype(jnp.bfloat16), 'dp', scatter_dimensio...  137 us
    reduce_scatter x1, waiting for transfers between devices, shards(): lax.psum_scatter(partials[1].astype(jnp.bfloat16), 'dp', scatter_dimensio...  137 us
    all_gather x1, waiting for transfers between devices, shards(): lax.all_gather(up_rows_grad, 'dp', axis=1, tiled=True)  83.4 us
    all_gather x1, waiting for transfers between devices, shards(): lax.all_gather(hidden_act, 'dp', axis=1, tiled=True)  57.9 us
    all_gather x1, waiting for transfers between devices, shards(): lax.all_gather(gate_rows_grad, 'dp', axis=1, tiled=True)  57.5 us
    all_to_all x1, waiting for transfers between devices, shards(): lax.all_to_all(outgoing[2], 'expert', split_axis=0, concat_axis=0, tiled=...  50.6 us
    all_to_all x1, waiting for transfers between devices, shards(): lax.all_to_all(term_down.reshape(groups, unit_piece, piece_width), 'exper...  46.6 us
    all_to_all x1, waiting for transfers between devices, shards(): lax.all_to_all(outgoing[1], 'expert', split_axis=0, concat_axis=0, tiled=...  45.1 us
  transfers between devices with their start and end apart: 12, of which 10 were waited for; matrix products, arithmetic and copies ran while one was open for 3% of the time, Pallas kernels for 0%

commit v1 on v0

v1 whole, which is shorter than its diff:
```python
import jax
import jax.numpy as jnp
from jax import lax
from jax.sharding import PartitionSpec as P


def product(left_rows, right_rows):
    return jnp.einsum("rd,fd->rf", left_rows, right_rows, preferred_element_type=jnp.float32)


def shards(
    rows_in, out_grad, route_weight, live_rows, expert_of_group, gate_weight, up_weight, down_weight
):
    groups = lax.axis_size("expert")
    n_dp = lax.axis_size("dp")
    chips = n_dp // 2
    experts_all, unit_piece, piece_width = gate_weight.shape
    units_all = unit_piece * groups
    row_count = rows_in.shape[0]
    half = row_count // 2
    share = half // chips
    core = lax.axis_index("dp") % 2
    partners = [(i, i ^ 1) for i in range(n_dp)]
    same_core = [[2 * i + c for i in range(chips)] for c in range(2)]

    outgoing = jnp.stack(
        [
            gate_weight[expert_of_group],
            up_weight[expert_of_group],
            down_weight[expert_of_group],
        ],
        axis=1,
    ).reshape(groups, 3 * unit_piece, piece_width)
    fetched = lax.all_to_all(outgoing, "expert", split_axis=0, concat_axis=0, tiled=True)
    fetched = fetched.reshape(groups, 3, unit_piece, piece_width)
    w_gate, w_up, w_down = (fetched[:, m].reshape(units_all, piece_width) for m in range(3))

    position = jnp.arange(row_count, dtype=jnp.int32)
    live_mask = (position < live_rows[0]).astype(jnp.float32)
    scaled = (out_grad.astype(jnp.float32) * (route_weight * live_mask)[:, None]).astype(
        jnp.bfloat16
    )

    def half_of(rows, which):
        return lax.dynamic_slice_in_dim(rows, which * half, half, axis=0)

    rows_mine, rows_other = half_of(rows_in, core), half_of(rows_in, 1 - core)
    scaled_mine, scaled_other = half_of(scaled, core), half_of(scaled, 1 - core)

    sent = jnp.concatenate(
        [
            product(rows_other, w_gate).astype(jnp.bfloat16),
            product(rows_other, w_up).astype(jnp.bfloat16),
            product(scaled_other, w_down).astype(jnp.bfloat16),
        ],
        axis=1,
    )
    got = lax.ppermute(sent, "dp", partners)
    got = [got[:, m * units_all : (m + 1) * units_all].astype(jnp.float32) for m in range(3)]
    paired = jnp.concatenate(
        [
            (product(rows_mine, w_gate) + got[0]).astype(jnp.bfloat16),
            (product(rows_mine, w_up) + got[1]).astype(jnp.bfloat16),
            (product(scaled_mine, w_down) + got[2]).astype(jnp.bfloat16),
        ],
        axis=1,
    ).reshape(chips, share, 3 * units_all)
    parts = lax.all_to_all(
        paired, "dp", split_axis=0, concat_axis=0, tiled=True, axis_index_groups=same_core
    )
    sums = jnp.sum(parts.astype(jnp.float32), axis=0)
    gate_sum, up_sum, hidden_grad = (
        sums[:, m * units_all : (m + 1) * units_all] for m in range(3)
    )
    sigmoid_gate = jax.nn.sigmoid(gate_sum)
    activated = gate_sum * sigmoid_gate
    hidden = jnp.concatenate(
        [
            hidden_grad * up_sum * sigmoid_gate * (1.0 + gate_sum * (1.0 - sigmoid_gate)),
            hidden_grad * activated,
            activated * up_sum,
        ],
        axis=1,
    ).astype(jnp.bfloat16)

    copies = jnp.broadcast_to(hidden[None], (chips, share, 3 * units_all))
    hidden_mine = lax.all_to_all(
        copies, "dp", split_axis=0, concat_axis=0, tiled=True, axis_index_groups=same_core
    ).reshape(half, 3 * units_all)
    hidden_other = lax.ppermute(hidden_mine, "dp", partners)

    def parts_of(hidden_half):
        return tuple(hidden_half[:, m * units_all : (m + 1) * units_all] for m in range(3))

    def term(mine, other, left, right):
        total = jnp.einsum("rf,rd->fd", mine, left, preferred_element_type=jnp.float32)
        total += jnp.einsum("rf,rd->fd", other, right, preferred_element_type=jnp.float32)
        return total.astype(jnp.bfloat16).reshape(groups, unit_piece, piece_width)

    gate_mine, up_mine, act_mine = parts_of(hidden_mine)
    gate_other, up_other, act_other = parts_of(hidden_other)
    terms = jnp.concatenate(
        [
            term(gate_mine, gate_other, rows_mine, rows_other),
            term(up_mine, up_other, rows_mine, rows_other),
            term(act_mine, act_other, scaled_mine, scaled_other),
        ],
        axis=1,
    )
    returned = lax.all_to_all(terms, "expert", split_axis=0, concat_axis=0, tiled=True)
    returned = returned.reshape(groups, 3, unit_piece, piece_width)

    def rows_grad_of(gate_half, up_half):
        return (
            jnp.dot(gate_half, w_gate, preferred_element_type=jnp.float32)
            + jnp.dot(up_half, w_up, preferred_element_type=jnp.float32)
        ).astype(jnp.bfloat16)

    grad_mine = rows_grad_of(gate_mine, up_mine)
    grad_other = rows_grad_of(gate_other, up_other)
    first = jnp.where(core == 0, grad_mine, grad_other)
    second = jnp.where(core == 0, grad_other, grad_mine)
    rows_grad = jnp.concatenate([first, second], axis=0)

    owner_table = (
        expert_of_group[:, None] == jnp.arange(experts_all, dtype=jnp.int32)[None, :]
    ).astype(jnp.bfloat16)
    gate_grad, up_grad, down_grad = (
        jnp.einsum(
            "ge,gfd->efd", owner_table, returned[:, m], preferred_element_type=jnp.float32
        ).astype(jnp.bfloat16)
        for m in range(3)
    )
    return (rows_grad, gate_grad, up_grad, down_grad)


def solution(mesh):
    return jax.shard_map(
        shards,
        mesh=mesh,
        in_specs=(
            P("expert", "dp"),
            P("expert", "dp"),
            P("expert"),
            P("expert"),
            P(),
            P(None, "expert", "dp"),
            P(None, "expert", "dp"),
            P(None, "expert", "dp"),
        ),
        out_specs=(
            P("expert", "dp"),
            P(None, "expert", "dp"),
            P(None, "expert", "dp"),
            P(None, "expert", "dp"),
        ),
        check_vma=False,
    )
```

time: 850 us -> 378 us (0.44)
  waiting for transfers between devices: 696 us -> 234 us
  blocking collectives: 0 us -> 70.5 us
  starting transfers between devices: 109 us -> 44.4 us
  between operations: 14.9 us -> 1.66 us
    reduce_scatter x3 -> x0, waiting for transfers between devices: 310 us -> none  [the longest x1 137 us: shards(): lax.psum_scatter(partials[0].astype(jnp.bfloat16), 'dp', scatter_dimensio...]
    all_gather x3 -> x0, waiting for transfers between devices: 199 us -> none  [the longest x1 83.4 us: shards(): lax.all_gather(up_rows_grad, 'dp', axis=1, tiled=True)]
    all_to_all x6 -> x2, starting transfers between devices: 109 us -> 37.7 us  [the longest x1 29.4 us: shards(): lax.all_to_all(outgoing, 'expert', split_axis=0, concat_axis=0, tiled=True)]
    all_to_all x0 -> x2, blocking collectives: none -> 70.5 us  [the longest x1 37.2 us: shards(): lax.all_to_all(paired, 'dp', split_axis=0, concat_axis=0, tiled=True, axi...]
    all_to_all x6 -> x2, waiting for transfers between devices: 187 us -> 227 us  [the longest x1 115 us: shards(): lax.all_to_all(outgoing, 'expert', split_axis=0, concat_axis=0, tiled=True)]
    dot_general x11 -> x19, matrix products: 18.2 us -> 10.3 us  [the longest x6 5.61 us: product(): jnp.einsum('rd,fd->rf', left_rows, right_rows, preferred_element_type=jnp...]
  transfers between devices with their start and end apart: 12 -> 4, of which waited for: 10 -> 4; matrix products, arithmetic and copies ran while one was open for 3% -> 1% of each run, Pallas kernels for 0% -> 0%
where the time goes in v1:
time: 378 us; the launch traced here: 377 us
  waiting for transfers between devices  234 us (62%)
  blocking collectives  70.5 us (19%)
  starting transfers between devices  44.4 us (12%)
  matrix products  10.3 us (3%)
  local copies, waits for them, and re-layouts  9.88 us (3%)
  other arithmetic  5.9 us (2%)
    all_to_all x1, waiting for transfers between devices, shards(): lax.all_to_all(outgoing, 'expert', split_axis=0, concat_axis=0, tiled=True)  115 us
    all_to_all x1, waiting for transfers between devices, shards(): lax.all_to_all(terms, 'expert', split_axis=0, concat_axis=0, tiled=True)  112 us
    all_to_all x1, blocking collectives, shards(): lax.all_to_all(paired, 'dp', split_axis=0, concat_axis=0, tiled=True, axi...  37.2 us
    all_to_all x1, blocking collectives, shards(): lax.all_to_all(copies, 'dp', split_axis=0, concat_axis=0, tiled=True, axi...  33.3 us
    all_to_all x1, starting transfers between devices, shards(): lax.all_to_all(outgoing, 'expert', split_axis=0, concat_axis=0, tiled=True)  29.4 us
    all_to_all x1, starting transfers between devices, shards(): lax.all_to_all(terms, 'expert', split_axis=0, concat_axis=0, tiled=True)  8.31 us
  transfers between devices with their start and end apart: 4, of which 4 were waited for; matrix products, arithmetic and copies ran while one was open for 1% of the time, Pallas kernels for 0%

profile of v1, /device:TPU:1, one launch (start us, length us, event | category | flops | bytes accessed | tf_op | source)
XLA Modules:
  0.0 376.6 jit_solution(17348318852525104469)
XLA Ops:
  0.6 0.7 compare_select_fusion
  2.3 1.6 gather_fusion.1
  3.9 1.6 gather_fusion
  5.6 1.2 pad_maximum_fusion.2
  6.7 29.4 %all-to-all-start = ((bf16[32,144,128]{2,1,0:T(8,128)(2,1)}), bf16[32,144,128]{2,1,0:T(8,128)(2,1)S(1)}, u32[]{:S(2)}, u32[]{:S(2)}) async-start(bf16[32,144,128]{2,1,0:T(8,128)(2,1)} %bitcast.3), calls=%async_computation | async-start | bytes 2359296 | tf_op jit(solution)/shard_map/all_to_all | solution.py:34
  37.0 114.6 %all-to-all-done = bf16[32,144,128]{2,1,0:T(8,128)(2,1)S(1)} async-done(((bf16[32,144,128]{2,1,0:T(8,128)(2,1)}), bf16[32,144,128]{2,1,0:T(8,128)(2,1)S(1)}, u32[]{:S(2)}, u32[]{:S(2)}) %all-to-all-start) | async-done | bytes 1179680 | tf_op jit(solution)/shard_map/all_to_all | solution.py:34
  152.8 1.6 pad_maximum_fusion
  154.4 2.6 collective-permute-start
  157.0 4.5 %collective-permute-done = bf16[256,4608]{1,0:T(8,128)(2,1)} collective-permute-done((bf16[256,4608]{1,0:T(8,128)(2,1)}, bf16[256,4608]{1,0:T(8,128)(2,1)}, u32[]{:S(2)}, u32[]{:S(2)}) %collective-permute-start) | collective-permute-done | bytes 2359328 | tf_op jit(solution)/shard_map/ppermute | solution.py:58
  161.5 1.5 add_convert_fusion
  163.0 1.5 add_convert_fusion.1
  164.5 1.5 add_convert_fusion.2
  166.2 37.2 %all_to_all.20 = bf16[16,16,4608]{2,1,0:T(8,128)(2,1)S(1)} all-to-all(bf16[16,16,4608]{2,1,0:T(8,128)(2,1)S(1)} %bitcast.46), channel_id=1, replica_groups={{0,2,4,6,8,10,12,14,16,18,20,22,24,26,28,30},{1,3,5,7,9,11,13,15,17,19,..., dimensions={0} | all-to-all | bytes 4718592 | tf_op jit(solution)/shard_map/all_to_all | solution.py:68
  204.1 33.3 %all_to_all.21 = bf16[16,16,4608]{2,1,0:T(8,128)(2,1)S(1)} all-to-all(bf16[16,16,4608]{2,1,0:T(8,128)(2,1)S(1)} %broadcast_in_dim.5), channel_id=1, replica_groups={{0,2,4,6,8,10,12,14,16,18,20,22,24,26,28,30},{1,3,5,7,9,11,13,15,17,19,..., dimensions={0} | all-to-all | bytes 4718592 | tf_op jit(solution)/shard_map/all_to_all | solution.py:87
  237.4 4.0 %collective-permute-start.1 = (bf16[256,4608]{1,0:T(8,128)(2,1)S(1)}, bf16[256,4608]{1,0:T(8,128)(2,1)S(1)}, u32[]{:S(2)}, u32[]{:S(2)}) collective-permute-start(bf16[256,4608]{1,0:T(8,128)(2,1)S(1)} %bitcast.40), channel_id=1, source_target_pairs={{0,1},{1,0},{2,3},{3,2},{4,5},{5,4},{6,7},{7,6},{8,9},{9,8},{10,11... | collective-permute-start | bytes 7077896 | tf_op jit(solution)/shard_map/ppermute | solution.py:90
  242.7 2.9 collective-permute-done.1
  247.0 1.1 pad_maximum_fusion.3
  248.1 8.3 %all-to-all-start.3 = ((bf16[32,144,128]{2,1,0:T(8,128)(2,1)}), bf16[32,144,128]{2,1,0:T(8,128)(2,1)}, u32[]{:S(2)}, u32[]{:S(2)}) async-start(bf16[32,144,128]{2,1,0:T(8,128)(2,1)} %pad_maximum_fusion.3), calls=%async_computation.3 | async-start | bytes 2359296 | tf_op jit(solution)/shard_map/all_to_all | solution.py:110
  257.1 0.9 copy-done.2
  259.5 112.1 %all-to-all-done.3 = bf16[32,144,128]{2,1,0:T(8,128)(2,1)} async-done(((bf16[32,144,128]{2,1,0:T(8,128)(2,1)}), bf16[32,144,128]{2,1,0:T(8,128)(2,1)}, u32[]{:S(2)}, u32[]{:S(2)}) %all-to-all-start.3) | async-done | bytes 1179680 | tf_op jit(solution)/shard_map/all_to_all | solution.py:110
  371.6 1.6 copy.16
  373.9 0.9 copy.17
  374.8 0.9 copy.18
  375.7 0.9 copy.19
  (46 shorter events, 8.5 us)
Async XLA Ops:
  0.6 1.0 copy-start
  5.5 31.3 %copy-start.9 = (f32[512]{0:T(512)S(1)}, f32[512]{0:T(512)}, u32[]{:S(2)}) copy-start(f32[512]{0:T(512)} %param.10) | copy-start | bytes 6148
  5.5 31.3 %copy-start.7 = (bf16[512,128]{1,0:T(8,128)(2,1)S(1)}, bf16[512,128]{1,0:T(8,128)(2,1)}, u32[]{:S(2)}) copy-start(bf16[512,128]{1,0:T(8,128)(2,1)} %param.9) | copy-start | bytes 393220
  6.7 145.0 %copy-start.3 = (bf16[512,128]{1,0:T(8,128)(2,1)S(1)}, bf16[512,128]{1,0:T(8,128)(2,1)}, u32[]{:S(2)}) copy-start(bf16[512,128]{1,0:T(8,128)(2,1)} %param.8) | copy-start | bytes 393220
  6.7 144.9 %all-to-all-start = ((bf16[32,144,128]{2,1,0:T(8,128)(2,1)}), bf16[32,144,128]{2,1,0:T(8,128)(2,1)S(1)}, u32[]{:S(2)}, u32[]{:S(2)}) async-start(bf16[32,144,128]{2,1,0:T(8,128)(2,1)} %bitcast.3), calls=%async_computation | async-start | bytes 2359296 | tf_op jit(solution)/shard_map/all_to_all | solution.py:34
  37.0 124.6 %copy-start.5 = (bf16[512,128]{1,0:T(8,128)(2,1)}, bf16[512,128]{1,0:T(8,128)(2,1)S(1)}, u32[]{:S(2)}) copy-start(bf16[512,128]{1,0:T(8,128)(2,1)S(1)} %multiply_convert_fusion) | copy-start | bytes 393220
  154.4 7.1 %collective-permute-start = (bf16[256,4608]{1,0:T(8,128)(2,1)}, bf16[256,4608]{1,0:T(8,128)(2,1)}, u32[]{:S(2)}, u32[]{:S(2)}) collective-permute-start(bf16[256,4608]{1,0:T(8,128)(2,1)} %pad_maximum_fusion), channel_id=1, source_target_pairs={{0,1},{1,0},{2,3},{3,2},{4,5},{5,4},{6,7},{7,6},{8,9},{9,8},{10,11... | collective-permute-start | bytes 7077896 | tf_op jit(solution)/shard_map/ppermute | solution.py:58
  204.1 37.4 %copy-start.6 = (bf16[512,128]{1,0:T(8,128)(2,1)S(1)}, bf16[512,128]{1,0:T(8,128)(2,1)}, u32[]{:S(2)}) copy-start(bf16[512,128]{1,0:T(8,128)(2,1)} %copy-done.5) | copy-start | bytes 393220
  204.1 37.8 %copy-start.4 = (bf16[512,128]{1,0:T(8,128)(2,1)S(1)}, bf16[512,128]{1,0:T(8,128)(2,1)}, u32[]{:S(2)}) copy-start(bf16[512,128]{1,0:T(8,128)(2,1)} %param.8) | copy-start | bytes 393220
  237.4 8.2 %collective-permute-start.1 = (bf16[256,4608]{1,0:T(8,128)(2,1)S(1)}, bf16[256,4608]{1,0:T(8,128)(2,1)S(1)}, u32[]{:S(2)}, u32[]{:S(2)}) collective-permute-start(bf16[256,4608]{1,0:T(8,128)(2,1)S(1)} %bitcast.40), channel_id=1, source_target_pairs={{0,1},{1,0},{2,3},{3,2},{4,5},{5,4},{6,7},{7,6},{8,9},{9,8},{10,11... | collective-permute-start | bytes 7077896 | tf_op jit(solution)/shard_map/ppermute | solution.py:90
  245.6 1.4 copy-start.1
  248.1 123.5 %all-to-all-start.3 = ((bf16[32,144,128]{2,1,0:T(8,128)(2,1)}), bf16[32,144,128]{2,1,0:T(8,128)(2,1)}, u32[]{:S(2)}, u32[]{:S(2)}) async-start(bf16[32,144,128]{2,1,0:T(8,128)(2,1)} %pad_maximum_fusion.3), calls=%async_computation.3 | async-start | bytes 2359296 | tf_op jit(solution)/shard_map/all_to_all | solution.py:110
  256.4 1.7 copy-start.2
  258.4 114.7 %copy-start.8 = (s32[32]{0:T(128)S(1)}, s32[32]{0:T(128)}, u32[]{:S(2)}) copy-start(s32[32]{0:T(128)} %param.12) | copy-start | bytes 388

commit v2 on v1

v2 whole, which is shorter than its diff:
```python
import functools

import jax
import jax.numpy as jnp
from jax import lax
from jax.experimental import pallas as pl
from jax.experimental.pallas import tpu as pltpu
from jax.sharding import PartitionSpec as P

LANES = 128
VMEM_LIMIT = 48 * 1024 * 1024


def product(left_rows, right_rows):
    return jnp.einsum("rd,fd->rf", left_rows, right_rows, preferred_element_type=jnp.float32)


def over_first(left, right):
    return lax.dot_general(
        left, right, (((0,), (0,)), ((), ())), preferred_element_type=jnp.float32
    )


def hidden_kernel(groups, piece, parts_ref, pieces_ref, grads_ref):
    units = groups * piece
    sums = parts_ref[0].astype(jnp.float32)
    for chip in range(1, parts_ref.shape[0]):
        sums += parts_ref[chip].astype(jnp.float32)
    gate_sum, up_sum, hidden_grad = (sums[:, m * units : (m + 1) * units] for m in range(3))
    sigmoid_gate = 1.0 / (1.0 + jnp.exp(-gate_sum))
    activated = gate_sum * sigmoid_gate
    hidden_act = activated * up_sum
    up_rows_grad = hidden_grad * activated
    gate_rows_grad = hidden_grad * up_sum * sigmoid_gate * (1.0 + gate_sum * (1.0 - sigmoid_gate))
    grads_ref[:, :units] = gate_rows_grad.astype(grads_ref.dtype)
    grads_ref[:, units:] = up_rows_grad.astype(grads_ref.dtype)
    spare = jnp.zeros((gate_sum.shape[0], 2 * LANES - 3 * piece), jnp.float32)
    for holder in range(groups):
        cut = slice(holder * piece, (holder + 1) * piece)
        pieces_ref[holder] = jnp.concatenate(
            [gate_rows_grad[:, cut], up_rows_grad[:, cut], hidden_act[:, cut], spare], axis=1
        ).astype(pieces_ref.dtype)


def pack_kernel(groups, tail, pieces_ref, packed_ref):
    per = LANES // tail
    packed_ref[:groups] = pieces_ref[:, :, :LANES]
    for block in range(groups // per):
        packed_ref[groups + block] = jnp.concatenate(
            [
                pieces_ref[block * per + k, :, LANES : LANES + tail].astype(jnp.float32)
                for k in range(per)
            ],
            axis=1,
        ).astype(packed_ref.dtype)


def weight_kernel(
    piece,
    tail,
    expert_ref,
    core_ref,
    rows_mine_ref,
    rows_other_ref,
    main_mine_ref,
    main_other_ref,
    rest_mine_ref,
    rest_other_ref,
    gate_ref,
    up_ref,
    down_ref,
    total_ref,
):
    step = pl.program_id(0)
    per = main_mine_ref.shape[1]
    half = rows_mine_ref.shape[2]

    @pl.when(step == 0)
    def _():
        total_ref[...] = jnp.zeros_like(total_ref)

    rest_mine = rest_mine_ref[:, 0].reshape(half, LANES)
    rest_other = rest_other_ref[:, 0].reshape(half, LANES)
    for k in range(per):
        expert = expert_ref[step * per + k]
        rows_mine, rows_other = rows_mine_ref[k, 0], rows_other_ref[k, 0]
        main = over_first(main_mine_ref[:, k].reshape(half, LANES), rows_mine)
        main += over_first(main_other_ref[:, k].reshape(half, LANES), rows_other)
        rest = over_first(rest_mine, rows_mine[:, LANES:])
        rest += over_first(rest_other, rows_other[:, LANES:])
        total_ref[expert, : 2 * piece] += main[: 2 * piece, :LANES]
        total_ref[expert, 2 * piece : LANES] += main[2 * piece :, LANES:]
        total_ref[expert, LANES:] += rest[k * tail : (k + 1) * tail]

    @pl.when(step == pl.num_programs(0) - 1)
    def _():
        gate_ref[...] = total_ref[:, :piece].astype(gate_ref.dtype)
        up_ref[...] = total_ref[:, piece : 2 * piece].astype(up_ref.dtype)
        down_ref[...] = total_ref[:, 2 * piece :].astype(down_ref.dtype)


def shards(
    rows_in, out_grad, route_weight, live_rows, expert_of_group, gate_weight, up_weight, down_weight
):
    groups = lax.axis_size("expert")
    n_dp = lax.axis_size("dp")
    chips = n_dp // 2
    experts_all, unit_piece, piece_width = gate_weight.shape
    units_all = unit_piece * groups
    row_count = rows_in.shape[0]
    half = row_count // 2
    share = half // chips
    tail = 3 * unit_piece - LANES
    per = LANES // tail
    core = lax.axis_index("dp") % 2
    partners = [(i, i ^ 1) for i in range(n_dp)]
    same_core = [[2 * i + c for i in range(chips)] for c in range(2)]

    def among_chips(blocks):
        return lax.all_to_all(
            blocks, "dp", split_axis=0, concat_axis=0, tiled=True, axis_index_groups=same_core
        )

    outgoing = jnp.stack(
        [
            gate_weight[expert_of_group],
            up_weight[expert_of_group],
            down_weight[expert_of_group],
        ],
        axis=1,
    ).reshape(groups, 3 * unit_piece, piece_width)
    fetched = lax.all_to_all(outgoing, "expert", split_axis=0, concat_axis=0, tiled=True)

    position = jnp.arange(row_count, dtype=jnp.int32)
    live_mask = (position < live_rows[0]).astype(jnp.float32)
    scaled = (out_grad.astype(jnp.float32) * (route_weight * live_mask)[:, None]).astype(
        jnp.bfloat16
    )
    both = jnp.concatenate([rows_in, scaled], axis=1)
    both, fetched = lax.optimization_barrier((both, fetched))
    rows_all = lax.all_gather(both, "expert", axis=0, tiled=True)
    fetched = fetched.reshape(groups, 3, unit_piece, piece_width)
    w_gate, w_up, w_down = (fetched[:, m].reshape(units_all, piece_width) for m in range(3))

    def half_of(rows, which):
        return lax.dynamic_slice_in_dim(rows, which * half, half, axis=0)

    rows_mine, rows_other = half_of(rows_in, core), half_of(rows_in, 1 - core)
    scaled_mine, scaled_other = half_of(scaled, core), half_of(scaled, 1 - core)

    sent = jnp.concatenate(
        [
            product(rows_other, w_gate).astype(jnp.bfloat16),
            product(rows_other, w_up).astype(jnp.bfloat16),
            product(scaled_other, w_down).astype(jnp.bfloat16),
        ],
        axis=1,
    )
    got = lax.ppermute(sent, "dp", partners)
    got = [got[:, m * units_all : (m + 1) * units_all].astype(jnp.float32) for m in range(3)]
    paired = jnp.concatenate(
        [
            (product(rows_mine, w_gate) + got[0]).astype(jnp.bfloat16),
            (product(rows_mine, w_up) + got[1]).astype(jnp.bfloat16),
            (product(scaled_mine, w_down) + got[2]).astype(jnp.bfloat16),
        ],
        axis=1,
    ).reshape(chips, share, 3 * units_all)
    parts = among_chips(paired)
    pieces, grads = pl.pallas_call(
        functools.partial(hidden_kernel, groups, unit_piece),
        out_shape=(
            jax.ShapeDtypeStruct((groups, share, 2 * LANES), jnp.bfloat16),
            jax.ShapeDtypeStruct((share, 2 * units_all), jnp.bfloat16),
        ),
        compiler_params=pltpu.CompilerParams(vmem_limit_bytes=VMEM_LIMIT),
    )(parts)

    pieces = lax.all_to_all(pieces, "expert", split_axis=0, concat_axis=0, tiled=True)
    packed_count = groups + groups // per
    packed = pl.pallas_call(
        functools.partial(pack_kernel, groups, tail),
        out_shape=jax.ShapeDtypeStruct((packed_count, share, LANES), jnp.bfloat16),
        compiler_params=pltpu.CompilerParams(vmem_limit_bytes=VMEM_LIMIT),
    )(pieces)
    packed_mine = among_chips(
        jnp.broadcast_to(packed[None], (chips, packed_count, share, LANES))
    )
    packed_other = lax.ppermute(packed_mine, "dp", partners)

    rows_by_half = rows_all.reshape(groups, 2, half, 2 * piece_width)
    main_spec = pl.BlockSpec((chips, per, share, LANES), lambda i, e, c: (0, i, 0, 0))
    rest_spec = pl.BlockSpec((chips, 1, share, LANES), lambda i, e, c: (0, groups + i, 0, 0))
    grad_shape = (experts_all, unit_piece, piece_width)
    grad_spec = pl.BlockSpec(grad_shape, lambda i, e, c: (0, 0, 0))
    gate_grad, up_grad, down_grad = pl.pallas_call(
        functools.partial(weight_kernel, unit_piece, tail),
        grid_spec=pltpu.PrefetchScalarGridSpec(
            num_scalar_prefetch=2,
            grid=(groups // per,),
            in_specs=[
                pl.BlockSpec((per, 1, half, 2 * piece_width), lambda i, e, c: (i, c[0], 0, 0)),
                pl.BlockSpec((per, 1, half, 2 * piece_width), lambda i, e, c: (i, 1 - c[0], 0, 0)),
                main_spec,
                main_spec,
                rest_spec,
                rest_spec,
            ],
            out_specs=(grad_spec, grad_spec, grad_spec),
            scratch_shapes=[
                pltpu.VMEM((experts_all, 3 * unit_piece, piece_width), jnp.float32)
            ],
        ),
        out_shape=tuple(jax.ShapeDtypeStruct(grad_shape, jnp.bfloat16) for _ in range(3)),
        compiler_params=pltpu.CompilerParams(vmem_limit_bytes=VMEM_LIMIT),
        cost_estimate=pl.CostEstimate(
            flops=4 * groups * row_count * LANES * 3 * LANES,
            bytes_accessed=16 * 1024 * 1024,
            transcendentals=0,
        ),
    )(
        expert_of_group,
        core.reshape(1).astype(jnp.int32),
        rows_by_half,
        rows_by_half,
        packed_mine,
        packed_other,
        packed_mine,
        packed_other,
    )

    grads_mine = among_chips(
        jnp.broadcast_to(grads[None], (chips, share, 2 * units_all))
    ).reshape(half, 2 * units_all)
    grads_other = lax.ppermute(grads_mine, "dp", partners)

    def rows_grad_of(grads_half):
        return (
            jnp.dot(grads_half[:, :units_all], w_gate, preferred_element_type=jnp.float32)
            + jnp.dot(grads_half[:, units_all:], w_up, preferred_element_type=jnp.float32)
        ).astype(jnp.bfloat16)

    grad_mine, grad_other = rows_grad_of(grads_mine), rows_grad_of(grads_other)
    first = jnp.where(core == 0, grad_mine, grad_other)
    second = jnp.where(core == 0, grad_other, grad_mine)
    rows_grad = jnp.concatenate([first, second], axis=0)
    return (rows_grad, gate_grad, up_grad, down_grad)


def solution(mesh):
    return jax.shard_map(
        shards,
        mesh=mesh,
        in_specs=(
            P("expert", "dp"),
            P("expert", "dp"),
            P("expert"),
            P("expert"),
            P(),
            P(None, "expert", "dp"),
            P(None, "expert", "dp"),
            P(None, "expert", "dp"),
        ),
        out_specs=(
            P("expert", "dp"),
            P(None, "expert", "dp"),
            P(None, "expert", "dp"),
            P(None, "expert", "dp"),
        ),
        check_vma=False,
    )
```

time: 378 us -> 350 us (0.926)
  waiting for transfers between devices: 234 us -> 131 us
  blocking collectives: 70.5 us -> 121 us
  between operations: 1.66 us -> 15 us
  Pallas kernels: 0 us -> 8.49 us
  starting transfers between devices: 44.4 us -> 50 us
    all_to_all x1, waiting for transfers between devices: 112 us -> 13.5 us  [among_chips(): lax.all_to_all(blocks, 'dp', split_axis=0, concat_axis=0, tiled=True, axi...]
    all_to_all x2 -> x3, blocking collectives: 70.5 us -> 121 us  [the longest x2 69 us: among_chips(): lax.all_to_all(blocks, 'dp', split_axis=0, concat_axis=0, tiled=True, axi...]
    ppermute x1 -> x2, starting transfers between devices: 4.03 us -> 13.4 us  [the longest x1 7.59 us: shards(): grads_other = lax.ppermute(grads_mine, 'dp', partners)]
    pallas_call x0 -> x3, Pallas kernels: none -> 8.49 us  [the longest x1 7.9 us: shards(): pl.pallas_call(functools.partial(weight_kernel, unit_piece, tail), grid_s...]
    all_to_all x1, starting transfers between devices: 8.31 us -> 4.41 us  [among_chips(): lax.all_to_all(blocks, 'dp', split_axis=0, concat_axis=0, tiled=True, axi...]
  transfers between devices with their start and end apart: 4 -> 6, of which waited for: 4 -> 4; matrix products, arithmetic and copies ran while one was open for 1% -> 5% of each run, Pallas kernels for 0% -> 0%
where the time goes in v2:
time: 350 us; the launch traced here: 349 us
  waiting for transfers between devices  131 us (37%)
  blocking collectives  121 us (35%)
  starting transfers between devices  50 us (14%)
  between operations  15 us (4%)
  matrix products  11.6 us (3%)
  Pallas kernels  8.49 us (2%)
  local copies, waits for them, and re-layouts  6.5 us (2%)
  other arithmetic  5.22 us (1%)
    all_to_all x1, waiting for transfers between devices, shards(): lax.all_to_all(outgoing, 'expert', split_axis=0, concat_axis=0, tiled=True)  113 us
    all_to_all x2, blocking collectives, among_chips(): lax.all_to_all(blocks, 'dp', split_axis=0, concat_axis=0, tiled=True, axi...  69 us
    all_to_all x1, blocking collectives, shards(): lax.all_to_all(pieces, 'expert', split_axis=0, concat_axis=0, tiled=True)  51.7 us
    all_to_all x1, starting transfers between devices, shards(): lax.all_to_all(outgoing, 'expert', split_axis=0, concat_axis=0, tiled=True)  29.4 us
    all_to_all x1, waiting for transfers between devices, among_chips(): lax.all_to_all(blocks, 'dp', split_axis=0, concat_axis=0, tiled=True, axi...  13.5 us
    pallas_call x1, Pallas kernels, shards(): pl.pallas_call(functools.partial(weight_kernel, unit_piece, tail), grid_s...  7.9 us
    ppermute x1, starting transfers between devices, shards(): grads_other = lax.ppermute(grads_mine, 'dp', partners)  7.59 us
  transfers between devices with their start and end apart: 6, of which 4 were waited for; matrix products, arithmetic and copies ran while one was open for 5% of the time, Pallas kernels for 0%

profile of v2, /device:TPU:1, one launch (start us, length us, event | category | flops | bytes accessed | tf_op | source)
XLA Modules:
  0.0 349.0 jit_solution(6875246938851122943)
XLA Ops:
  8.8 1.6 gather_fusion.1
  11.1 1.1 pad_maximum_fusion.2
  12.2 29.4 %all-to-all-start = ((bf16[32,144,128]{2,1,0:T(8,128)(2,1)}), bf16[32,144,128]{2,1,0:T(8,128)(2,1)S(1)}, u32[]{:S(2)}, u32[]{:S(2)}) async-start(bf16[32,144,128]{2,1,0:T(8,128)(2,1)} %bitcast.4), calls=%async_computation | async-start | bytes 2359296 | tf_op jit(solution)/shard_map/all_to_all | solution.py:132
  43.9 113.2 %all-to-all-done = bf16[32,144,128]{2,1,0:T(8,128)(2,1)S(1)} async-done(((bf16[32,144,128]{2,1,0:T(8,128)(2,1)}), bf16[32,144,128]{2,1,0:T(8,128)(2,1)S(1)}, u32[]{:S(2)}, u32[]{:S(2)}) %all-to-all-start) | async-done | bytes 1179680 | tf_op jit(solution)/shard_map/all_to_all | solution.py:132
  157.3 0.8 copy-done.6
  159.2 1.6 pad_maximum_fusion
  160.9 2.7 collective-permute-start
  163.6 4.5 %collective-permute-done = bf16[256,4608]{1,0:T(8,128)(2,1)} collective-permute-done((bf16[256,4608]{1,0:T(8,128)(2,1)}, bf16[256,4608]{1,0:T(8,128)(2,1)}, u32[]{:S(2)}, u32[]{:S(2)}) %collective-permute-start) | collective-permute-done | bytes 2359328 | tf_op jit(solution)/shard_map/ppermute | solution.py:159
  168.1 1.5 add_convert_fusion
  169.6 1.5 add_convert_fusion.1
  171.1 1.5 add_convert_fusion.2
  172.8 37.2 %all_to_all.25.parts_ref = bf16[16,16,4608]{2,1,0:T(8,128)(2,1)S(1)} all-to-all(bf16[16,16,4608]{2,1,0:T(8,128)(2,1)S(1)} %bitcast.26), channel_id=1, replica_groups={{0,2,4,6,8,10,12,14,16,18,20,22,24,26,28,30},{1,3,5,7,9,11,13,15,17,19,..., dimensions={0} | all-to-all | bytes 4718592 | tf_op jit(solution)/shard_map/all_to_all | solution.py:120
  210.5 51.7 %all_to_all.26.pieces_ref = bf16[32,16,256]{2,1,0:T(8,128)(2,1)S(1)} all-to-all(bf16[32,16,256]{2,1,0:T(8,128)(2,1)S(1)} %get-tuple-element.14), channel_id=1, replica_groups=mesh['expert'=32,'dp'=32] {'expert'}, dimensions={0} | all-to-all | bytes 524288 | tf_op jit(solution)/shard_map/all_to_all | solution.py:179
  262.8 31.7 %all_to_all.27.main_mine_ref.rest_mine_ref = bf16[16,36,16,128]{3,2,1,0:T(8,128)(2,1)S(1)} all-to-all(bf16[16,36,16,128]{3,2,1,0:T(8,128)(2,1)S(1)} %broadcast_in_dim.8), channel_id=1, replica_groups={{0,2,4,6,8,10,12,14,16,18,20,22,24,26,28,30},{1,3,5,7,9,11,13,15,17,19,..., dimensions={0} | all-to-all | bytes 4718592 | tf_op jit(solution)/shard_map/all_to_all | solution.py:120
  294.6 1.4 broadcast_in_dim.7
  295.9 4.4 %all-to-all-start.2 = ((bf16[16,16,3072]{2,1,0:T(8,128)(2,1)}), bf16[16,16,3072]{2,1,0:T(8,128)(2,1)}, u32[]{:S(2)}, u32[]{:S(2)}) async-start(bf16[16,16,3072]{2,1,0:T(8,128)(2,1)} %broadcast_in_dim.7), calls=%async_computation.2 | async-start | bytes 3145728 | tf_op jit(solution)/shard_map/all_to_all | solution.py:120
  300.3 5.8 %collective-permute-start.2 = (bf16[16,36,16,128]{3,2,1,0:T(8,128)(2,1)S(1)}, bf16[16,36,16,128]{3,2,1,0:T(8,128)(2,1)}, u32[]{:S(2)}, u32[]{:S(2)}) collective-permute-start(bf16[16,36,16,128]{3,2,1,0:T(8,128)(2,1)S(1)} %all_to_all.27.main_mine_ref.rest_mine_ref), channel_id=1, source_target_pairs={{0,1},{1,0},{2,3},{3,2},{4,5},{5,4},{6,7},{7,6},{8,9},{9,8},{10,11... | collective-permute-start | bytes 7077896 | tf_op jit(solution)/shard_map/ppermute | solution.py:189
  306.2 13.5 %all-to-all-done.2 = bf16[16,16,3072]{2,1,0:T(8,128)(2,1)} async-done(((bf16[16,16,3072]{2,1,0:T(8,128)(2,1)}), bf16[16,16,3072]{2,1,0:T(8,128)(2,1)}, u32[]{:S(2)}, u32[]{:S(2)}) %all-to-all-start.2) | async-done | bytes 1572896 | tf_op jit(solution)/shard_map/all_to_all | solution.py:120
  319.6 7.6 %collective-permute-start.1 = (bf16[256,3072]{1,0:T(8,128)(2,1)}, bf16[256,3072]{1,0:T(8,128)(2,1)}, u32[]{:S(2)}, u32[]{:S(2)}) collective-permute-start(bf16[256,3072]{1,0:T(8,128)(2,1)} %bitcast.10), channel_id=1, source_target_pairs={{0,1},{1,0},{2,3},{3,2},{4,5},{5,4},{6,7},{7,6},{8,9},{9,8},{10,11... | collective-permute-start | bytes 4718600 | tf_op jit(solution)/shard_map/ppermute | solution.py:235
  327.2 1.5 fusion.6
  328.7 1.5 fusion
  330.6 1.5 fusion.2
  332.1 1.5 broadcast_select_fusion.1
  334.3 7.9 %shard_map.113 = (bf16[32,48,128]{2,1,0:T(8,128)(2,1)}, bf16[32,48,128]{2,1,0:T(8,128)(2,1)}, bf16[32,48,128]{2,1,0:T(8,128)(2,1)}) custom-call(s32[32]{0:T(128)S(1)} %copy-done.1, s32[1]{0:T(128)} %bitcast.11.core_ref, bf16[32,2,256,256]{3,2,1,0:T(8,128)(2,1)} %bitcast.24, bf16[32,2,256,256]{3,2,1,0:T(8,128)(2,1)} %bitcast.25, ...), custom_call_target="tpu_custom_call" | custom-call | flops 3221225472 | bytes 16777216 | tf_op jit(solution)/shard_map/pallas_call | solution.py:196
  (42 shorter events, 7.3 us)
Async XLA Ops:
  7.2 1.0 copy-start
  7.2 3.3 copy-start.8
  12.2 30.1 %copy-start.10 = (f32[512]{0:T(512)S(1)}, f32[512]{0:T(512)}, u32[]{:S(2)}) copy-start(f32[512]{0:T(512)} %param.10) | copy-start | bytes 6148
  12.2 30.1 %copy-start.9 = (bf16[512,128]{1,0:T(8,128)(2,1)S(1)}, bf16[512,128]{1,0:T(8,128)(2,1)}, u32[]{:S(2)}) copy-start(bf16[512,128]{1,0:T(8,128)(2,1)} %param.9) | copy-start | bytes 393220
  12.2 30.9 %copy-start.2 = (bf16[512,128]{1,0:T(8,128)(2,1)S(1)}, bf16[512,128]{1,0:T(8,128)(2,1)}, u32[]{:S(2)}) copy-start(bf16[512,128]{1,0:T(8,128)(2,1)} %param.8) | copy-start | bytes 393220
  12.2 144.9 %all-to-all-start = ((bf16[32,144,128]{2,1,0:T(8,128)(2,1)}), bf16[32,144,128]{2,1,0:T(8,128)(2,1)S(1)}, u32[]{:S(2)}, u32[]{:S(2)}) async-start(bf16[32,144,128]{2,1,0:T(8,128)(2,1)} %bitcast.4), calls=%async_computation | async-start | bytes 2359296 | tf_op jit(solution)/shard_map/all_to_all | solution.py:132
  41.7 292.6 %all-gather.2.cloned.1.call-start = ((), (), s32[]{:S(2)}) async-start(), calls=%async_computation.5 | async-start | bytes 8650752 | tf_op jit(solution)/shard_map/all_gather | solution.py:141
  42.5 0.7 copy-start.5
  157.2 0.9 copy-start.6
  157.2 1.3 copy-start.3
  159.2 8.9 %copy-start.7 = (bf16[512,128]{1,0:T(8,128)(2,1)S(1)}, bf16[512,128]{1,0:T(8,128)(2,1)}, u32[]{:S(2)}) copy-start(bf16[512,128]{1,0:T(8,128)(2,1)} %copy-done.5) | copy-start | bytes 393220
  160.9 8.7 %copy-start.4 = (bf16[512,128]{1,0:T(8,128)(2,1)S(1)}, bf16[512,128]{1,0:T(8,128)(2,1)}, u32[]{:S(2)}) copy-start(bf16[512,128]{1,0:T(8,128)(2,1)} %param.8) | copy-start | bytes 393220
  160.9 7.2 %collective-permute-start = (bf16[256,4608]{1,0:T(8,128)(2,1)}, bf16[256,4608]{1,0:T(8,128)(2,1)}, u32[]{:S(2)}, u32[]{:S(2)}) collective-permute-start(bf16[256,4608]{1,0:T(8,128)(2,1)} %pad_maximum_fusion), channel_id=1, source_target_pairs={{0,1},{1,0},{2,3},{3,2},{4,5},{5,4},{6,7},{7,6},{8,9},{9,8},{10,11... | collective-permute-start | bytes 7077896 | tf_op jit(solution)/shard_map/ppermute | solution.py:159
  295.9 23.7 %all-to-all-start.2 = ((bf16[16,16,3072]{2,1,0:T(8,128)(2,1)}), bf16[16,16,3072]{2,1,0:T(8,128)(2,1)}, u32[]{:S(2)}, u32[]{:S(2)}) async-start(bf16[16,16,3072]{2,1,0:T(8,128)(2,1)} %broadcast_in_dim.7), calls=%async_computation.2 | async-start | bytes 3145728 | tf_op jit(solution)/shard_map/all_to_all | solution.py:120
  300.3 33.9 %collective-permute-start.2 = (bf16[16,36,16,128]{3,2,1,0:T(8,128)(2,1)S(1)}, bf16[16,36,16,128]{3,2,1,0:T(8,128)(2,1)}, u32[]{:S(2)}, u32[]{:S(2)}) collective-permute-start(bf16[16,36,16,128]{3,2,1,0:T(8,128)(2,1)S(1)} %all_to_all.27.main_mine_ref.rest_mine_ref), channel_id=1, source_target_pairs={{0,1},{1,0},{2,3},{3,2},{4,5},{5,4},{6,7},{7,6},{8,9},{9,8},{10,11... | collective-permute-start | bytes 7077896 | tf_op jit(solution)/shard_map/ppermute | solution.py:189
  319.6 10.9 %collective-permute-start.1 = (bf16[256,3072]{1,0:T(8,128)(2,1)}, bf16[256,3072]{1,0:T(8,128)(2,1)}, u32[]{:S(2)}, u32[]{:S(2)}) collective-permute-start(bf16[256,3072]{1,0:T(8,128)(2,1)} %bitcast.10), channel_id=1, source_target_pairs={{0,1},{1,0},{2,3},{3,2},{4,5},{5,4},{6,7},{7,6},{8,9},{9,8},{10,11... | collective-permute-start | bytes 4718600 | tf_op jit(solution)/shard_map/ppermute | solution.py:235
  330.2 4.0 %copy-start.1 = (s32[32]{0:T(128)S(1)}, s32[32]{0:T(128)}, u32[]{:S(2)}) copy-start(s32[32]{0:T(128)} %expert_ref.1) | copy-start | bytes 388
Sparse Core Ops, SparseCore 0:
  157.3 146.3 all-gather.1

commit v3 on v2

--- a/solution.py
+++ b/solution.py
@@ -8,17 +8,60 @@
 from jax.sharding import PartitionSpec as P
 
 LANES = 128
-VMEM_LIMIT = 48 * 1024 * 1024
-
-
-def product(left_rows, right_rows):
-    return jnp.einsum("rd,fd->rf", left_rows, right_rows, preferred_element_type=jnp.float32)
+VMEM_LIMIT = 20 * 1024 * 1024
+LARGE_VMEM_LIMIT = 60 * 1024 * 1024
 
 
 def over_first(left, right):
     return lax.dot_general(
         left, right, (((0,), (0,)), ((), ())), preferred_element_type=jnp.float32
     )
+
+
+def gather_kernel(piece, expert_ref, gate_ref, up_ref, down_ref, out_ref, sems):
+    copies = []
+    for group in range(out_ref.shape[0]):
+        for m, weight_ref in enumerate((gate_ref, up_ref, down_ref)):
+            copy = pltpu.make_async_copy(
+                weight_ref.at[expert_ref[group]],
+                out_ref.at[group, pl.ds(m * piece, piece)],
+                sems.at[group * 3 + m],
+            )
+            copy.start()
+            copies.append(copy)
+    for copy in copies:
+        copy.wait()
+
+
+def flat(weights_ref, m, piece):
+    groups, _, width = weights_ref.shape
+    return weights_ref[:, m * piece : (m + 1) * piece, :].reshape(groups * piece, width)
+
+
+def products(piece, which, rows_ref, scaled_ref, weights_ref):
+    half = rows_ref.shape[0] // 2
+    start = pl.multiple_of(which * half, half)
+    rows, scaled = rows_ref[pl.ds(start, half)], scaled_ref[pl.ds(start, half)]
+    for m, left in enumerate((rows, rows, scaled)):
+        yield m, lax.dot_general(
+            left,
+            flat(weights_ref, m, piece),
+            (((1,), (1,)), ((), ())),
+            preferred_element_type=jnp.float32,
+        )
+
+
+def sent_kernel(piece, core_ref, rows_ref, scaled_ref, weights_ref, out_ref):
+    units = out_ref.shape[1] // 3
+    for m, summed in products(piece, 1 - core_ref[0], rows_ref, scaled_ref, weights_ref):
+        out_ref[:, m * units : (m + 1) * units] = summed.astype(out_ref.dtype)
+
+
+def paired_kernel(piece, core_ref, rows_ref, scaled_ref, weights_ref, got_ref, out_ref):
+    units = out_ref.shape[1] // 3
+    for m, summed in products(piece, core_ref[0], rows_ref, scaled_ref, weights_ref):
+        cut = slice(m * units, (m + 1) * units)
+        out_ref[:, cut] = (summed + got_ref[:, cut].astype(jnp.float32)).astype(out_ref.dtype)
 
 
 def hidden_kernel(groups, piece, parts_ref, pieces_ref, grads_ref):
@@ -32,27 +75,68 @@
     hidden_act = activated * up_sum
     up_rows_grad = hidden_grad * activated
     gate_rows_grad = hidden_grad * up_sum * sigmoid_gate * (1.0 + gate_sum * (1.0 - sigmoid_gate))
-    grads_ref[:, :units] = gate_rows_grad.astype(grads_ref.dtype)
-    grads_ref[:, units:] = up_rows_grad.astype(grads_ref.dtype)
-    spare = jnp.zeros((gate_sum.shape[0], 2 * LANES - 3 * piece), jnp.float32)
+    blocks = units // LANES
+    for k in range(blocks):
+        cut = slice(k * LANES, (k + 1) * LANES)
+        grads_ref[k] = gate_rows_grad[:, cut].astype(grads_ref.dtype)
+        grads_ref[blocks + k] = up_rows_grad[:, cut].astype(grads_ref.dtype)
+    _, fold, width = pieces_ref.shape
+    spare = jnp.zeros((fold, width - 6 * piece), jnp.float32)
     for holder in range(groups):
         cut = slice(holder * piece, (holder + 1) * piece)
         pieces_ref[holder] = jnp.concatenate(
-            [gate_rows_grad[:, cut], up_rows_grad[:, cut], hidden_act[:, cut], spare], axis=1
+            [
+                array[rows, cut]
+                for rows in (slice(0, fold), slice(fold, 2 * fold))
+                for array in (gate_rows_grad, up_rows_grad, hidden_act)
+            ]
+            + [spare],
+            axis=1,
         ).astype(pieces_ref.dtype)
 
 
-def pack_kernel(groups, tail, pieces_ref, packed_ref):
+def pack_kernel(groups, tail, pieces_ref, grads_ref, copies_ref):
     per = LANES // tail
-    packed_ref[:groups] = pieces_ref[:, :, :LANES]
+    width = LANES + tail
+    rows = []
+    for group in range(groups):
+        folded = pieces_ref[group].astype(jnp.float32)
+        rows.append(jnp.concatenate([folded[:, :width], folded[:, width : 2 * width]], axis=0))
+    for group in range(groups):
+        copies_ref[0, group] = rows[group][:, :LANES].astype(copies_ref.dtype)
     for block in range(groups // per):
-        packed_ref[groups + block] = jnp.concatenate(
-            [
-                pieces_ref[block * per + k, :, LANES : LANES + tail].astype(jnp.float32)
-                for k in range(per)
-            ],
-            axis=1,
-        ).astype(packed_ref.dtype)
+        copies_ref[0, groups + block] = jnp.concatenate(
+            [rows[block * per + k][:, LANES:] for k in range(per)], axis=1
+        ).astype(copies_ref.dtype)
+    copies_ref[0, groups + groups // per :] = grads_ref[...]
+    for chip in range(1, copies_ref.shape[0]):
+        copies_ref[chip] = copies_ref[0]
+
+
+def rows_kernel(piece, core_ref, mine_ref, other_ref, weights_ref, out_ref, total_ref):
+    m = pl.program_id(0)
+    half = out_ref.shape[0] // 2
+    blocks = mine_ref.shape[1]
+    groups, width = weights_ref.shape[0], weights_ref.shape[2]
+    start = pl.multiple_of(m * piece, piece)
+    weights = weights_ref[:, pl.ds(start, piece), :].reshape(groups * piece, width)
+    for ref, which in ((mine_ref, core_ref[0]), (other_ref, 1 - core_ref[0])):
+        total = jnp.zeros((half, width), jnp.float32)
+        for k in range(blocks):
+            total += jnp.dot(
+                ref[:, k].reshape(half, LANES),
+                weights[k * LANES : (k + 1) * LANES],
+                preferred_element_type=jnp.float32,
+            )
+        rows = pl.ds(pl.multiple_of(which * half, half), half)
+
+        @pl.when(m == 0)
+        def _():
+            total_ref[rows] = total
+
+        @pl.when(m == 1)
+        def _():
+            out_ref[rows] = (total_ref[rows] + total).astype(out_ref.dtype)
 
 
 def weight_kernel(
@@ -121,14 +205,19 @@
             blocks, "dp", split_axis=0, concat_axis=0, tiled=True, axis_index_groups=same_core
         )
 
-    outgoing = jnp.stack(
-        [
-            gate_weight[expert_of_group],
-            up_weight[expert_of_group],
-            down_weight[expert_of_group],
-        ],
-        axis=1,
-    ).reshape(groups, 3 * unit_piece, piece_width)
+    in_vmem = pl.BlockSpec(memory_space=pltpu.VMEM)
+    in_smem = pl.BlockSpec(memory_space=pltpu.SMEM)
+    in_place = pl.BlockSpec(memory_space=pl.ANY)
+    roomy = pltpu.CompilerParams(vmem_limit_bytes=VMEM_LIMIT)
+    core_index = core.reshape(1).astype(jnp.int32)
+
+    outgoing = pl.pallas_call(
+        functools.partial(gather_kernel, unit_piece),
+        in_specs=[in_smem, in_place, in_place, in_place],
+        out_specs=in_vmem,
+        out_shape=jax.ShapeDtypeStruct((groups, 3 * unit_piece, piece_width), jnp.bfloat16),
+        scratch_shapes=[pltpu.SemaphoreType.DMA((3 * groups,))],
+    )(expert_of_group, gate_weight, up_weight, down_weight)
     fetched = lax.all_to_all(outgoing, "expert", split_axis=0, concat_axis=0, tiled=True)
 
     position = jnp.arange(row_count, dtype=jnp.int32)
@@ -139,54 +228,79 @@
     both = jnp.concatenate([rows_in, scaled], axis=1)
     both, fetched = lax.optimization_barrier((both, fetched))
     rows_all = lax.all_gather(both, "expert", axis=0, tiled=True)
-    fetched = fetched.reshape(groups, 3, unit_piece, piece_width)
-    w_gate, w_up, w_down = (fetched[:, m].reshape(units_all, piece_width) for m in range(3))
-
-    def half_of(rows, which):
-        return lax.dynamic_slice_in_dim(rows, which * half, half, axis=0)
-
-    rows_mine, rows_other = half_of(rows_in, core), half_of(rows_in, 1 - core)
-    scaled_mine, scaled_other = half_of(scaled, core), half_of(scaled, 1 - core)
-
-    sent = jnp.concatenate(
-        [
-            product(rows_other, w_gate).astype(jnp.bfloat16),
-            product(rows_other, w_up).astype(jnp.bfloat16),
-            product(scaled_other, w_down).astype(jnp.bfloat16),
-        ],
-        axis=1,
-    )
+
+    product_flops = 2 * half * 3 * units_all * piece_width
+    product_bytes = 2 * (half + groups * piece_width) * 3 * unit_piece * 16
+    sent = pl.pallas_call(
+        functools.partial(sent_kernel, unit_piece),
+        in_specs=[in_smem, in_vmem, in_vmem, in_vmem],
+        out_specs=in_vmem,
+        out_shape=jax.ShapeDtypeStruct((half, 3 * units_all), jnp.bfloat16),
+        compiler_params=roomy,
+        cost_estimate=pl.CostEstimate(
+            flops=product_flops, bytes_accessed=product_bytes, transcendentals=0
+        ),
+    )(core_index, rows_in, scaled, fetched)
     got = lax.ppermute(sent, "dp", partners)
-    got = [got[:, m * units_all : (m + 1) * units_all].astype(jnp.float32) for m in range(3)]
-    paired = jnp.concatenate(
-        [
-            (product(rows_mine, w_gate) + got[0]).astype(jnp.bfloat16),
-            (product(rows_mine, w_up) + got[1]).astype(jnp.bfloat16),
-            (product(scaled_mine, w_down) + got[2]).astype(jnp.bfloat16),
-        ],
-        axis=1,
-    ).reshape(chips, share, 3 * units_all)
+    paired = pl.pallas_call(
+        functools.partial(paired_kernel, unit_piece),
+        in_specs=[in_smem, in_vmem, in_vmem, in_vmem, in_vmem],
+        out_specs=in_vmem,
+        out_shape=jax.ShapeDtypeStruct((half, 3 * units_all), jnp.bfloat16),
+        compiler_params=roomy,
+        cost_estimate=pl.CostEstimate(
+            flops=product_flops, bytes_accessed=product_bytes, transcendentals=0
+        ),
+    )(core_index, rows_in, scaled, fetched, got).reshape(chips, share, 3 * units_all)
     parts = among_chips(paired)
+    grad_blocks = 2 * units_all // LANES
     pieces, grads = pl.pallas_call(
         functools.partial(hidden_kernel, groups, unit_piece),
         out_shape=(
-            jax.ShapeDtypeStruct((groups, share, 2 * LANES), jnp.bfloat16),
-            jax.ShapeDtypeStruct((share, 2 * units_all), jnp.bfloat16),
-        ),
-        compiler_params=pltpu.CompilerParams(vmem_limit_bytes=VMEM_LIMIT),
+            jax.ShapeDtypeStruct((groups, share // 2, 3 * LANES), jnp.bfloat16),
+            jax.ShapeDtypeStruct((grad_blocks, share, LANES), jnp.bfloat16),
+        ),
+        compiler_params=roomy,
     )(parts)
 
     pieces = lax.all_to_all(pieces, "expert", split_axis=0, concat_axis=0, tiled=True)
     packed_count = groups + groups // per
-    packed = pl.pallas_call(
+    copies = pl.pallas_call(
         functools.partial(pack_kernel, groups, tail),
-        out_shape=jax.ShapeDtypeStruct((packed_count, share, LANES), jnp.bfloat16),
-        compiler_params=pltpu.CompilerParams(vmem_limit_bytes=VMEM_LIMIT),
-    )(pieces)
-    packed_mine = among_chips(
-        jnp.broadcast_to(packed[None], (chips, packed_count, share, LANES))
-    )
-    packed_other = lax.ppermute(packed_mine, "dp", partners)
+        out_shape=jax.ShapeDtypeStruct(
+            (chips, packed_count + grad_blocks, share, LANES), jnp.bfloat16
+        ),
+        compiler_params=roomy,
+    )(pieces, grads)
+    hidden_mine = among_chips(copies)
+    hidden_other = lax.ppermute(hidden_mine, "dp", partners)
+
+    gate_blocks = grad_blocks // 2
+    first = packed_count // gate_blocks
+    grads_spec = pl.BlockSpec(
+        (chips, gate_blocks, share, LANES), lambda m, c: (0, first + m, 0, 0)
+    )
+    rows_grad = pl.pallas_call(
+        functools.partial(rows_kernel, unit_piece),
+        grid_spec=pltpu.PrefetchScalarGridSpec(
+            num_scalar_prefetch=1,
+            grid=(2,),
+            in_specs=[
+                grads_spec,
+                grads_spec,
+                pl.BlockSpec(fetched.shape, lambda m, c: (0, 0, 0)),
+            ],
+            out_specs=pl.BlockSpec((row_count, piece_width), lambda m, c: (0, 0)),
+            scratch_shapes=[pltpu.VMEM((row_count, piece_width), jnp.float32)],
+        ),
+        out_shape=jax.ShapeDtypeStruct((row_count, piece_width), jnp.bfloat16),
+        compiler_params=pltpu.CompilerParams(vmem_limit_bytes=LARGE_VMEM_LIMIT),
+        cost_estimate=pl.CostEstimate(
+            flops=4 * row_count * units_all * piece_width,
+            bytes_accessed=5 * 1024 * 1024,
+            transcendentals=0,
+        ),
+    )(core_index, hidden_mine, hidden_other, fetched)
 
     rows_by_half = rows_all.reshape(groups, 2, half, 2 * piece_width)
     main_spec = pl.BlockSpec((chips, per, share, LANES), lambda i, e, c: (0, i, 0, 0))
@@ -212,7 +326,7 @@
             ],
         ),
         out_shape=tuple(jax.ShapeDtypeStruct(grad_shape, jnp.bfloat16) for _ in range(3)),
-        compiler_params=pltpu.CompilerParams(vmem_limit_bytes=VMEM_LIMIT),
+        compiler_params=pltpu.CompilerParams(vmem_limit_bytes=LARGE_VMEM_LIMIT),
         cost_estimate=pl.CostEstimate(
             flops=4 * groups * row_count * LANES * 3 * LANES,
             bytes_accessed=16 * 1024 * 1024,
@@ -220,30 +334,15 @@
         ),
     )(
         expert_of_group,
-        core.reshape(1).astype(jnp.int32),
+        core_index,
         rows_by_half,
         rows_by_half,
-        packed_mine,
-        packed_other,
-        packed_mine,
-        packed_other,
-    )
-
-    grads_mine = among_chips(
-        jnp.broadcast_to(grads[None], (chips, share, 2 * units_all))
-    ).reshape(half, 2 * units_all)
-    grads_other = lax.ppermute(grads_mine, "dp", partners)
-
-    def rows_grad_of(grads_half):
-        return (
-            jnp.dot(grads_half[:, :units_all], w_gate, preferred_element_type=jnp.float32)
-            + jnp.dot(grads_half[:, units_all:], w_up, preferred_element_type=jnp.float32)
-        ).astype(jnp.bfloat16)
-
-    grad_mine, grad_other = rows_grad_of(grads_mine), rows_grad_of(grads_other)
-    first = jnp.where(core == 0, grad_mine, grad_other)
-    second = jnp.where(core == 0, grad_other, grad_mine)
-    rows_grad = jnp.concatenate([first, second], axis=0)
+        hidden_mine,
+        hidden_other,
+        hidden_mine,
+        hidden_other,
+    )
+
     return (rows_grad, gate_grad, up_grad, down_grad)
 
 

time: 350 us -> 332 us (0.949)
  blocking collectives: 121 us -> 134 us
  starting transfers between devices: 50 us -> 37.3 us
  matrix products: 11.6 us -> 0 us
  Pallas kernels: 8.49 us -> 19.8 us
  local copies, waits for them, and re-layouts: 6.5 us -> 0.02 us
  waiting for transfers between devices: 131 us -> 125 us
  other arithmetic: 5.22 us -> 0.87 us
    all_to_all x2, blocking collectives: 69 us -> 88.4 us  [among_chips(): lax.all_to_all(blocks, 'dp', split_axis=0, concat_axis=0, tiled=True, axi...]
    all_to_all x1 -> x0, waiting for transfers between devices: 13.5 us -> none  [among_chips(): lax.all_to_all(blocks, 'dp', split_axis=0, concat_axis=0, tiled=True, axi...]
    dot_general x10 -> x0, matrix products: 11.6 us -> none  [the longest x6 5.62 us: product(): jnp.einsum('rd,fd->rf', left_rows, right_rows, preferred_element_type=jnp...]
    pallas_call x0 -> x4, Pallas kernels: none -> 10.3 us  [the longest x1 4.59 us: shards(): pl.pallas_call(functools.partial(rows_kernel, unit_piece), grid_spec=pltp...]
    ppermute x2 -> x1, starting transfers between devices: 13.4 us -> 5.39 us  [shards(): hidden_other = lax.ppermute(hidden_mine, 'dp', partners)]
    all_to_all x1, blocking collectives: 51.7 us -> 45.4 us  [shards(): lax.all_to_all(pieces, 'expert', split_axis=0, concat_axis=0, tiled=True)]
    ppermute x2 -> x1, waiting for transfers between devices: 0.34 us -> 6.52 us  [shards(): hidden_other = lax.ppermute(hidden_mine, 'dp', partners)]
    all_to_all x1 -> x0, starting transfers between devices: 4.41 us -> none  [among_chips(): lax.all_to_all(blocks, 'dp', split_axis=0, concat_axis=0, tiled=True, axi...]
  transfers between devices with their start and end apart: 6 -> 4, of which waited for: 4 -> 3; matrix products, arithmetic and copies ran while one was open for 5% -> 0% of each run, Pallas kernels for 0% -> 2%
where the time goes in v3:
time: 332 us; the launch traced here: 331 us
  blocking collectives  134 us (40%)
  waiting for transfers between devices  125 us (38%)
  starting transfers between devices  37.3 us (11%)
  Pallas kernels  19.8 us (6%)
  between operations  14.8 us (4%)
    all_to_all x1, waiting for transfers between devices, shards(): lax.all_to_all(outgoing, 'expert', split_axis=0, concat_axis=0, tiled=True)  114 us
    all_to_all x2, blocking collectives, among_chips(): lax.all_to_all(blocks, 'dp', split_axis=0, concat_axis=0, tiled=True, axi...  88.4 us
    all_to_all x1, blocking collectives, shards(): lax.all_to_all(pieces, 'expert', split_axis=0, concat_axis=0, tiled=True)  45.4 us
    all_to_all x1, starting transfers between devices, shards(): lax.all_to_all(outgoing, 'expert', split_axis=0, concat_axis=0, tiled=True)  29.3 us
    pallas_call x1, Pallas kernels, shards(): pl.pallas_call(functools.partial(weight_kernel, unit_piece, tail), grid_s...  8.4 us
  transfers between devices with their start and end apart: 4, of which 3 were waited for; matrix products, arithmetic and copies ran while one was open for 0% of the time, Pallas kernels for 2%

profile of v3, /device:TPU:1, one launch (start us, length us, event | category | flops | bytes accessed | tf_op | source)
XLA Modules:
  0.0 331.3 jit_solution(14489991794559229740)
XLA Ops:
  7.2 0.0 copy-start.4
  7.2 0.0 copy-start.3
  7.2 0.0 copy-start.1
  7.2 4.2 %shard_map.111 = bf16[32,144,128]{2,1,0:T(8,128)(2,1)} custom-call(s32[32]{0:T(128)} %expert_ref.3, bf16[32,48,128]{2,1,0:T(8,128)(2,1)} %gate_ref.1, bf16[32,48,128]{2,1,0:T(8,128)(2,1)} %up_ref.1, bf16[32,48,128]{2,1,0:T(8,128)(2,1)} %down_ref.1), custom_call_target="tpu_custom_call" | custom-call | tf_op jit(solution)/shard_map/pallas_call | solution.py:214
  11.4 29.3 %all-to-all-start = ((bf16[32,144,128]{2,1,0:T(8,128)(2,1)}), bf16[32,144,128]{2,1,0:T(8,128)(2,1)S(1)}, u32[]{:S(2)}, u32[]{:S(2)}) async-start(bf16[32,144,128]{2,1,0:T(8,128)(2,1)} %shard_map.111), calls=%async_computation | async-start | bytes 2359296 | tf_op jit(solution)/shard_map/all_to_all | solution.py:221
  40.7 0.0 all-gather.2.cloned.1.call-start
  41.4 0.0 copy-done.4
  41.4 0.1 multiply_convert_fusion.scaled_ref
  41.5 0.7 pad_maximum_fusion
  42.3 113.9 %all-to-all-done.weights_ref = bf16[32,144,128]{2,1,0:T(8,128)(2,1)S(1)} async-done(((bf16[32,144,128]{2,1,0:T(8,128)(2,1)}), bf16[32,144,128]{2,1,0:T(8,128)(2,1)S(1)}, u32[]{:S(2)}, u32[]{:S(2)}) %all-to-all-start) | async-done | bytes 1179680 | tf_op jit(solution)/shard_map/all_to_all | solution.py:221
  156.1 0.0 all-gather.2.cloned.1.call-update
  156.2 0.8 shard_map.112
  157.0 2.6 collective-permute-start
  159.6 4.1 %collective-permute-done.got_ref = bf16[256,4608]{1,0:T(8,128)(2,1)S(1)} collective-permute-done((bf16[256,4608]{1,0:T(8,128)(2,1)S(1)}, bf16[256,4608]{1,0:T(8,128)(2,1)S(1)}, u32[]{:S(2)}, u32[]{:S(2)}) %collective-permute-start) | collective-permute-done | bytes 2359328 | tf_op jit(solution)/shard_map/ppermute | solution.py:244
  163.7 0.8 shard_map.113
  164.5 37.2 %all_to_all.20.parts_ref = bf16[16,16,4608]{2,1,0:T(8,128)(2,1)S(1)} all-to-all(bf16[16,16,4608]{2,1,0:T(8,128)(2,1)S(1)} %bitcast.5), channel_id=1, replica_groups={{0,2,4,6,8,10,12,14,16,18,20,22,24,26,28,30},{1,3,5,7,9,11,13,15,17,19,..., dimensions={0} | all-to-all | bytes 4718592 | tf_op jit(solution)/shard_map/all_to_all | solution.py:204
  201.8 0.5 shard_map.114
  202.3 45.4 %all_to_all.21.pieces_ref = bf16[32,8,384]{2,1,0:T(8,128)(2,1)S(1)} all-to-all(bf16[32,8,384]{2,1,0:T(8,128)(2,1)S(1)} %get-tuple-element.12), channel_id=1, replica_groups=mesh['expert'=32,'dp'=32] {'expert'}, dimensions={0} | all-to-all | bytes 393216 | tf_op jit(solution)/shard_map/all_to_all | solution.py:266
  247.7 0.6 shard_map.115
  248.3 51.2 %all_to_all.22.mine_ref.main_mine_ref.rest_mine_ref = bf16[16,60,16,128]{3,2,1,0:T(8,128)(2,1)S(1)} all-to-all(bf16[16,60,16,128]{3,2,1,0:T(8,128)(2,1)S(1)} %shard_map.115), channel_id=1, replica_groups={{0,2,4,6,8,10,12,14,16,18,20,22,24,26,28,30},{1,3,5,7,9,11,13,15,17,19,..., dimensions={0} | all-to-all | bytes 7864320 | tf_op jit(solution)/shard_map/all_to_all | solution.py:204
  299.5 5.4 %collective-permute-start.1 = (bf16[16,60,16,128]{3,2,1,0:T(8,128)(2,1)S(1)}, bf16[16,60,16,128]{3,2,1,0:T(8,128)(2,1)}, u32[]{:S(2)}, u32[]{:S(2)}) collective-permute-start(bf16[16,60,16,128]{3,2,1,0:T(8,128)(2,1)S(1)} %all_to_all.22.mine_ref.main_mine_ref.rest_mine_ref), channel_id=1, source_target_pairs={{0,1},{1,0},{2,3},{3,2},{4,5},{5,4},{6,7},{7,6},{8,9},{9,8},{10,11... | collective-permute-start | bytes 11796488 | tf_op jit(solution)/shard_map/ppermute | solution.py:276
  304.9 6.5 %collective-permute-done.1.other_ref.main_other_ref.rest_other_ref = bf16[16,60,16,128]{3,2,1,0:T(8,128)(2,1)} collective-permute-done((bf16[16,60,16,128]{3,2,1,0:T(8,128)(2,1)S(1)}, bf16[16,60,16,128]{3,2,1,0:T(8,128)(2,1)}, u32[]{:S(2)}, u32[]{:S(2)}) %collective-permute-start.1) | collective-permute-done | bytes 3932192 | tf_op jit(solution)/shard_map/ppermute | solution.py:276
  311.4 4.6 %shard_map.116 = bf16[512,128]{1,0:T(8,128)(2,1)} custom-call(s32[1]{0:T(128)} %bitcast.core_ref, bf16[16,60,16,128]{3,2,1,0:T(8,128)(2,1)} %copy-done.2, bf16[16,60,16,128]{3,2,1,0:T(8,128)(2,1)} %collective-permute-done.1.other_ref.main_other_ref.rest_other_ref, bf16[32,144,128]{2,1,0:T(8,128)(2,1)} %copy-done), custom_call_target="tpu_custom_call" | custom-call | flops 402653184 | bytes 5242880 | tf_op jit(solution)/shard_map/pallas_call | solution.py:283
  316.0 8.4 %shard_map.117 = (bf16[32,48,128]{2,1,0:T(8,128)(2,1)}, bf16[32,48,128]{2,1,0:T(8,128)(2,1)}, bf16[32,48,128]{2,1,0:T(8,128)(2,1)}) custom-call(s32[32]{0:T(128)} %expert_ref.3, s32[1]{0:T(128)} %bitcast.core_ref, bf16[32,2,256,256]{3,2,1,0:T(8,128)(2,1)} %bitcast.6, bf16[32,2,256,256]{3,2,1,0:T(8,128)(2,1)} %bitcast.7, bf16[16,60,16,128]{3,2,1,0:T(8,128)(2,1)} %copy-done.2, ...), custom_call_target="tpu_custom_call" | custom-call | flops 3221225472 | bytes 16777216 | tf_op jit(solution)/shard_map/pallas_call | solution.py:310
  (8 shorter events, 0.0 us)
Async XLA Ops:
  7.2 34.2 %copy-start.4 = (f32[512]{0:T(512)S(1)}, f32[512]{0:T(512)}, u32[]{:S(2)}) copy-start(f32[512]{0:T(512)} %param.10) | copy-start | bytes 6148
  7.2 34.2 %copy-start.3 = (bf16[512,128]{1,0:T(8,128)(2,1)S(1)}, bf16[512,128]{1,0:T(8,128)(2,1)}, u32[]{:S(2)}) copy-start(bf16[512,128]{1,0:T(8,128)(2,1)} %param.9) | copy-start | bytes 393220
  7.2 34.4 %copy-start.1 = (bf16[512,128]{1,0:T(8,128)(2,1)S(1)}, bf16[512,128]{1,0:T(8,128)(2,1)}, u32[]{:S(2)}) copy-start(bf16[512,128]{1,0:T(8,128)(2,1)} %rows_ref.3) | copy-start | bytes 393220
  11.4 144.8 %all-to-all-start = ((bf16[32,144,128]{2,1,0:T(8,128)(2,1)}), bf16[32,144,128]{2,1,0:T(8,128)(2,1)S(1)}, u32[]{:S(2)}, u32[]{:S(2)}) async-start(bf16[32,144,128]{2,1,0:T(8,128)(2,1)} %shard_map.111), calls=%async_computation | async-start | bytes 2359296 | tf_op jit(solution)/shard_map/all_to_all | solution.py:221
  40.7 275.3 %all-gather.2.cloned.1.call-start = ((), (), s32[]{:S(2)}) async-start(), calls=%async_computation.4 | async-start | bytes 8650752 | tf_op jit(solution)/shard_map/all_gather | solution.py:230
  156.1 8.4 %copy-start = (bf16[32,144,128]{2,1,0:T(8,128)(2,1)}, bf16[32,144,128]{2,1,0:T(8,128)(2,1)S(1)}, u32[]{:S(2)}) copy-start(bf16[32,144,128]{2,1,0:T(8,128)(2,1)S(1)} %all-to-all-done.weights_ref) | copy-start | bytes 3538948
  157.0 6.8 %collective-permute-start = (bf16[256,4608]{1,0:T(8,128)(2,1)S(1)}, bf16[256,4608]{1,0:T(8,128)(2,1)S(1)}, u32[]{:S(2)}, u32[]{:S(2)}) collective-permute-start(bf16[256,4608]{1,0:T(8,128)(2,1)S(1)} %shard_map.112), channel_id=1, source_target_pairs={{0,1},{1,0},{2,3},{3,2},{4,5},{5,4},{6,7},{7,6},{8,9},{9,8},{10,11... | collective-permute-start | bytes 7077896 | tf_op jit(solution)/shard_map/ppermute | solution.py:244
  299.5 11.9 %copy-start.2 = (bf16[16,60,16,128]{3,2,1,0:T(8,128)(2,1)}, bf16[16,60,16,128]{3,2,1,0:T(8,128)(2,1)S(1)}, u32[]{:S(2)}) copy-start(bf16[16,60,16,128]{3,2,1,0:T(8,128)(2,1)S(1)} %all_to_all.22.mine_ref.main_mine_ref.rest_mine_ref) | copy-start | bytes 11796484
  299.5 11.9 %collective-permute-start.1 = (bf16[16,60,16,128]{3,2,1,0:T(8,128)(2,1)S(1)}, bf16[16,60,16,128]{3,2,1,0:T(8,128)(2,1)}, u32[]{:S(2)}, u32[]{:S(2)}) collective-permute-start(bf16[16,60,16,128]{3,2,1,0:T(8,128)(2,1)S(1)} %all_to_all.22.mine_ref.main_mine_ref.rest_mine_ref), channel_id=1, source_target_pairs={{0,1},{1,0},{2,3},{3,2},{4,5},{5,4},{6,7},{7,6},{8,9},{9,8},{10,11... | collective-permute-start | bytes 11796488 | tf_op jit(solution)/shard_map/ppermute | solution.py:276
Sparse Core Ops, SparseCore 0:
  156.3 140.9 all-gather.1

commit v4 on v3

--- a/solution.py
+++ b/solution.py
@@ -9,7 +9,8 @@
 
 LANES = 128
 VMEM_LIMIT = 20 * 1024 * 1024
-LARGE_VMEM_LIMIT = 60 * 1024 * 1024
+LARGE_VMEM_LIMIT = 50 * 1024 * 1024
+GATHER_VMEM_LIMIT = 60 * 1024 * 1024
 
 
 def over_first(left, right):
@@ -18,19 +19,17 @@
     )
 
 
-def gather_kernel(piece, expert_ref, gate_ref, up_ref, down_ref, out_ref, sems):
-    copies = []
-    for group in range(out_ref.shape[0]):
-        for m, weight_ref in enumerate((gate_ref, up_ref, down_ref)):
-            copy = pltpu.make_async_copy(
-                weight_ref.at[expert_ref[group]],
-                out_ref.at[group, pl.ds(m * piece, piece)],
-                sems.at[group * 3 + m],
-            )
-            copy.start()
-            copies.append(copy)
+def gather_kernel(piece, expert_ref, gate_ref, up_ref, down_ref, out_ref, weights_ref, sems):
+    copies = [
+        pltpu.make_async_copy(weight_ref, weights_ref.at[m], sems.at[m])
+        for m, weight_ref in enumerate((gate_ref, up_ref, down_ref))
+    ]
     for copy in copies:
+        copy.start()
+    for m, copy in enumerate(copies):
         copy.wait()
+        for group in range(out_ref.shape[0]):
+            out_ref[group, m * piece : (m + 1) * piece] = weights_ref[m, expert_ref[group]]
 
 
 def flat(weights_ref, m, piece):
@@ -113,74 +112,76 @@
         copies_ref[chip] = copies_ref[0]
 
 
-def rows_kernel(piece, core_ref, mine_ref, other_ref, weights_ref, out_ref, total_ref):
-    m = pl.program_id(0)
-    half = out_ref.shape[0] // 2
-    blocks = mine_ref.shape[1]
-    groups, width = weights_ref.shape[0], weights_ref.shape[2]
-    start = pl.multiple_of(m * piece, piece)
-    weights = weights_ref[:, pl.ds(start, piece), :].reshape(groups * piece, width)
-    for ref, which in ((mine_ref, core_ref[0]), (other_ref, 1 - core_ref[0])):
-        total = jnp.zeros((half, width), jnp.float32)
+def turned_kernel(tail, piece, hidden_ref, weights_ref, turned_ref, rows_ref):
+    groups, _, half = turned_ref.shape
+    per = LANES // tail
+    for block in range(groups // per):
+        rest = hidden_ref[:, groups + block].reshape(half, LANES).T
+        for k in range(per):
+            group = block * per + k
+            turned_ref[group, :LANES] = hidden_ref[:, group].reshape(half, LANES).T
+            turned_ref[group, LANES:] = rest[k * tail : (k + 1) * tail]
+    first = groups + groups // per
+    blocks = (hidden_ref.shape[1] - first) // 2
+    total = jnp.zeros(rows_ref.shape, jnp.float32)
+    for m in range(2):
+        weights = flat(weights_ref, m, piece)
         for k in range(blocks):
             total += jnp.dot(
-                ref[:, k].reshape(half, LANES),
+                hidden_ref[:, first + m * blocks + k].reshape(half, LANES),
                 weights[k * LANES : (k + 1) * LANES],
                 preferred_element_type=jnp.float32,
             )
-        rows = pl.ds(pl.multiple_of(which * half, half), half)
-
-        @pl.when(m == 0)
-        def _():
-            total_ref[rows] = total
-
-        @pl.when(m == 1)
-        def _():
-            out_ref[rows] = (total_ref[rows] + total).astype(out_ref.dtype)
+    rows_ref[...] = total.astype(rows_ref.dtype)
 
 
 def weight_kernel(
     piece,
-    tail,
+    steps,
     expert_ref,
     core_ref,
-    rows_mine_ref,
-    rows_other_ref,
-    main_mine_ref,
-    main_other_ref,
-    rest_mine_ref,
-    rest_other_ref,
+    mine_ref,
+    other_ref,
+    rows_ref,
     gate_ref,
     up_ref,
     down_ref,
+    turned_ref,
+    held_ref,
     total_ref,
+    sems,
 ):
-    step = pl.program_id(0)
-    per = main_mine_ref.shape[1]
-    half = rows_mine_ref.shape[2]
-
-    @pl.when(step == 0)
-    def _():
-        total_ref[...] = jnp.zeros_like(total_ref)
-
-    rest_mine = rest_mine_ref[:, 0].reshape(half, LANES)
-    rest_other = rest_other_ref[:, 0].reshape(half, LANES)
-    for k in range(per):
-        expert = expert_ref[step * per + k]
-        rows_mine, rows_other = rows_mine_ref[k, 0], rows_other_ref[k, 0]
-        main = over_first(main_mine_ref[:, k].reshape(half, LANES), rows_mine)
-        main += over_first(main_other_ref[:, k].reshape(half, LANES), rows_other)
-        rest = over_first(rest_mine, rows_mine[:, LANES:])
-        rest += over_first(rest_other, rows_other[:, LANES:])
-        total_ref[expert, : 2 * piece] += main[: 2 * piece, :LANES]
-        total_ref[expert, 2 * piece : LANES] += main[2 * piece :, LANES:]
-        total_ref[expert, LANES:] += rest[k * tail : (k + 1) * tail]
-
-    @pl.when(step == pl.num_programs(0) - 1)
-    def _():
-        gate_ref[...] = total_ref[:, :piece].astype(gate_ref.dtype)
-        up_ref[...] = total_ref[:, piece : 2 * piece].astype(up_ref.dtype)
-        down_ref[...] = total_ref[:, 2 * piece :].astype(down_ref.dtype)
+    groups = rows_ref.shape[0]
+    per = groups // steps
+    sides = [
+        pltpu.make_async_copy(ref, turned_ref.at[i], sems.at[steps + i])
+        for i, ref in enumerate((mine_ref, other_ref))
+    ]
+    for copy in sides:
+        copy.start()
+    copies = []
+    for step in range(steps):
+        cut = pl.ds(step * per, per)
+        copies.append(pltpu.make_async_copy(rows_ref.at[cut], held_ref.at[cut], sems.at[step]))
+        copies[step].start()
+    total_ref[...] = jnp.zeros_like(total_ref)
+    core = core_ref[0]
+    for copy in sides:
+        copy.wait()
+    for group in range(groups):
+        if group % per == 0:
+            copies[group // per].wait()
+        expert = expert_ref[group]
+        term = jnp.dot(
+            turned_ref[0, group], held_ref[group, core], preferred_element_type=jnp.float32
+        )
+        term += jnp.dot(
+            turned_ref[1, group], held_ref[group, 1 - core], preferred_element_type=jnp.float32
+        )
+        total_ref[expert, : 2 * piece] += term[: 2 * piece, :LANES]
+        total_ref[expert, 2 * piece :] += term[2 * piece :, LANES:]
+    for m, out_ref in enumerate((gate_ref, up_ref, down_ref)):
+        out_ref[...] = total_ref[:, m * piece : (m + 1) * piece].astype(out_ref.dtype)
 
 
 def shards(
@@ -216,7 +217,11 @@
         in_specs=[in_smem, in_place, in_place, in_place],
         out_specs=in_vmem,
         out_shape=jax.ShapeDtypeStruct((groups, 3 * unit_piece, piece_width), jnp.bfloat16),
-        scratch_shapes=[pltpu.SemaphoreType.DMA((3 * groups,))],
+        scratch_shapes=[
+            pltpu.VMEM((3, *gate_weight.shape), jnp.bfloat16),
+            pltpu.SemaphoreType.DMA((3,)),
+        ],
+        compiler_params=pltpu.CompilerParams(vmem_limit_bytes=GATHER_VMEM_LIMIT),
     )(expert_of_group, gate_weight, up_weight, down_weight)
     fetched = lax.all_to_all(outgoing, "expert", split_axis=0, concat_axis=0, tiled=True)
 
@@ -275,73 +280,51 @@
     hidden_mine = among_chips(copies)
     hidden_other = lax.ppermute(hidden_mine, "dp", partners)
 
-    gate_blocks = grad_blocks // 2
-    first = packed_count // gate_blocks
-    grads_spec = pl.BlockSpec(
-        (chips, gate_blocks, share, LANES), lambda m, c: (0, first + m, 0, 0)
+    def turned(hidden):
+        return pl.pallas_call(
+            functools.partial(turned_kernel, tail, unit_piece),
+            out_shape=(
+                jax.ShapeDtypeStruct((groups, 3 * unit_piece, half), jnp.bfloat16),
+                jax.ShapeDtypeStruct((half, piece_width), jnp.bfloat16),
+            ),
+            compiler_params=roomy,
+            cost_estimate=pl.CostEstimate(
+                flops=2 * row_count * units_all * piece_width,
+                bytes_accessed=7 * 1024 * 1024,
+                transcendentals=0,
+            ),
+        )(hidden, fetched)
+
+    turned_mine, grad_mine = turned(hidden_mine)
+    turned_other, grad_other = turned(hidden_other)
+    rows_grad = jnp.concatenate(
+        [
+            jnp.where(core == 0, grad_mine, grad_other),
+            jnp.where(core == 0, grad_other, grad_mine),
+        ],
+        axis=0,
     )
-    rows_grad = pl.pallas_call(
-        functools.partial(rows_kernel, unit_piece),
-        grid_spec=pltpu.PrefetchScalarGridSpec(
-            num_scalar_prefetch=1,
-            grid=(2,),
-            in_specs=[
-                grads_spec,
-                grads_spec,
-                pl.BlockSpec(fetched.shape, lambda m, c: (0, 0, 0)),
-            ],
-            out_specs=pl.BlockSpec((row_count, piece_width), lambda m, c: (0, 0)),
-            scratch_shapes=[pltpu.VMEM((row_count, piece_width), jnp.float32)],
-        ),
-        out_shape=jax.ShapeDtypeStruct((row_count, piece_width), jnp.bfloat16),
-        compiler_params=pltpu.CompilerParams(vmem_limit_bytes=LARGE_VMEM_LIMIT),
-        cost_estimate=pl.CostEstimate(
-            flops=4 * row_count * units_all * piece_width,
-            bytes_accessed=5 * 1024 * 1024,
-            transcendentals=0,
-        ),
-    )(core_index, hidden_mine, hidden_other, fetched)
 
     rows_by_half = rows_all.reshape(groups, 2, half, 2 * piece_width)
-    main_spec = pl.BlockSpec((chips, per, share, LANES), lambda i, e, c: (0, i, 0, 0))
-    rest_spec = pl.BlockSpec((chips, 1, share, LANES), lambda i, e, c: (0, groups + i, 0, 0))
     grad_shape = (experts_all, unit_piece, piece_width)
-    grad_spec = pl.BlockSpec(grad_shape, lambda i, e, c: (0, 0, 0))
     gate_grad, up_grad, down_grad = pl.pallas_call(
-        functools.partial(weight_kernel, unit_piece, tail),
-        grid_spec=pltpu.PrefetchScalarGridSpec(
-            num_scalar_prefetch=2,
-            grid=(groups // per,),
-            in_specs=[
-                pl.BlockSpec((per, 1, half, 2 * piece_width), lambda i, e, c: (i, c[0], 0, 0)),
-                pl.BlockSpec((per, 1, half, 2 * piece_width), lambda i, e, c: (i, 1 - c[0], 0, 0)),
-                main_spec,
-                main_spec,
-                rest_spec,
-                rest_spec,
-            ],
-            out_specs=(grad_spec, grad_spec, grad_spec),
-            scratch_shapes=[
-                pltpu.VMEM((experts_all, 3 * unit_piece, piece_width), jnp.float32)
-            ],
-        ),
+        functools.partial(weight_kernel, unit_piece, 8),
+        in_specs=[in_smem, in_smem, in_place, in_place, in_place],
+        out_specs=(in_vmem,) * 3,
         out_shape=tuple(jax.ShapeDtypeStruct(grad_shape, jnp.bfloat16) for _ in range(3)),
+        scratch_shapes=[
+            pltpu.VMEM((2, *turned_mine.shape), jnp.bfloat16),
+            pltpu.VMEM(rows_by_half.shape, jnp.bfloat16),
+            pltpu.VMEM((experts_all, 3 * unit_piece, piece_width), jnp.float32),
+            pltpu.SemaphoreType.DMA((8 + 2,)),
+        ],
         compiler_params=pltpu.CompilerParams(vmem_limit_bytes=LARGE_VMEM_LIMIT),
         cost_estimate=pl.CostEstimate(
             flops=4 * groups * row_count * LANES * 3 * LANES,
-            bytes_accessed=16 * 1024 * 1024,
+            bytes_accessed=12 * 1024 * 1024,
             transcendentals=0,
         ),
-    )(
-        expert_of_group,
-        core_index,
-        rows_by_half,
-        rows_by_half,
-        hidden_mine,
-        hidden_other,
-        hidden_mine,
-        hidden_other,
-    )
+    )(expert_of_group, core_index, turned_mine, turned_other, rows_by_half)
 
     return (rows_grad, gate_grad, up_grad, down_grad)
 

time: 332 us -> 328 us (0.988)
    pallas_call x2 -> x3, Pallas kernels: 13 us -> 12 us  [the longest x1 6.4 us: shards(): pl.pallas_call(functools.partial(weight_kernel, unit_piece, 8), in_specs=...]
  transfers between devices with their start and end apart: 4 -> 4, of which waited for: 3 -> 3; matrix products, arithmetic and copies ran while one was open for 0% -> 0% of each run, Pallas kernels for 2% -> 3%
where the time goes in v4:
time: 328 us
  blocking collectives  133 us (41%)
  waiting for transfers between devices  122 us (37%)
  starting transfers between devices  37.3 us (11%)
  Pallas kernels  17.8 us (5%)
  between operations  14.9 us (5%)
    all_to_all x1, waiting for transfers between devices, shards(): lax.all_to_all(outgoing, 'expert', split_axis=0, concat_axis=0, tiled=True)  114 us
    all_to_all x2, blocking collectives, among_chips(): lax.all_to_all(blocks, 'dp', split_axis=0, concat_axis=0, tiled=True, axi...  87.4 us
    all_to_all x1, blocking collectives, shards(): lax.all_to_all(pieces, 'expert', split_axis=0, concat_axis=0, tiled=True)  45.4 us
    all_to_all x1, starting transfers between devices, shards(): lax.all_to_all(outgoing, 'expert', split_axis=0, concat_axis=0, tiled=True)  29.3 us
  transfers between devices with their start and end apart: 4, of which 3 were waited for; matrix products, arithmetic and copies ran while one was open for 0% of the time, Pallas kernels for 3%

profile of v4, /device:TPU:1, one launch (start us, length us, event | category | flops | bytes accessed | tf_op | source)
XLA Modules:
  0.0 327.7 jit_solution(14876247193983537825)
XLA Ops:
  7.2 3.1 shard_map.111
  10.3 29.3 %all-to-all-start = ((bf16[32,144,128]{2,1,0:T(8,128)(2,1)}), bf16[32,144,128]{2,1,0:T(8,128)(2,1)S(1)}, u32[]{:S(2)}, u32[]{:S(2)}) async-start(bf16[32,144,128]{2,1,0:T(8,128)(2,1)} %shard_map.111), calls=%async_computation | async-start | bytes 2359296 | tf_op jit(solution)/shard_map/all_to_all | solution.py:226
  39.6 0.0 all-gather.2.cloned.1.call-start
  40.3 0.1 multiply_convert_fusion.scaled_ref
  40.5 0.7 pad_maximum_fusion
  41.2 113.9 %all-to-all-done.weights_ref = bf16[32,144,128]{2,1,0:T(8,128)(2,1)S(1)} async-done(((bf16[32,144,128]{2,1,0:T(8,128)(2,1)}), bf16[32,144,128]{2,1,0:T(8,128)(2,1)S(1)}, u32[]{:S(2)}, u32[]{:S(2)}) %all-to-all-start) | async-done | bytes 1179680 | tf_op jit(solution)/shard_map/all_to_all | solution.py:226
  155.1 0.0 all-gather.2.cloned.1.call-update
  155.1 0.8 shard_map.112
  155.9 2.6 collective-permute-start
  158.5 4.1 %collective-permute-done.got_ref = bf16[256,4608]{1,0:T(8,128)(2,1)S(1)} collective-permute-done((bf16[256,4608]{1,0:T(8,128)(2,1)S(1)}, bf16[256,4608]{1,0:T(8,128)(2,1)S(1)}, u32[]{:S(2)}, u32[]{:S(2)}) %collective-permute-start) | collective-permute-done | bytes 2359328 | tf_op jit(solution)/shard_map/ppermute | solution.py:249
  162.7 0.8 shard_map.113
  163.5 37.2 %all_to_all.20.parts_ref = bf16[16,16,4608]{2,1,0:T(8,128)(2,1)S(1)} all-to-all(bf16[16,16,4608]{2,1,0:T(8,128)(2,1)S(1)} %bitcast.5), channel_id=1, replica_groups={{0,2,4,6,8,10,12,14,16,18,20,22,24,26,28,30},{1,3,5,7,9,11,13,15,17,19,..., dimensions={0} | all-to-all | bytes 4718592 | tf_op jit(solution)/shard_map/all_to_all | solution.py:205
  200.7 0.5 shard_map.114
  201.2 45.4 %all_to_all.21.pieces_ref = bf16[32,8,384]{2,1,0:T(8,128)(2,1)S(1)} all-to-all(bf16[32,8,384]{2,1,0:T(8,128)(2,1)S(1)} %get-tuple-element.16), channel_id=1, replica_groups=mesh['expert'=32,'dp'=32] {'expert'}, dimensions={0} | all-to-all | bytes 393216 | tf_op jit(solution)/shard_map/all_to_all | solution.py:271
  246.6 0.6 shard_map.115
  247.2 50.1 %all_to_all.22.hidden_ref = bf16[16,60,16,128]{3,2,1,0:T(8,128)(2,1)} all-to-all(bf16[16,60,16,128]{3,2,1,0:T(8,128)(2,1)S(1)} %shard_map.115), channel_id=1, replica_groups={{0,2,4,6,8,10,12,14,16,18,20,22,24,26,28,30},{1,3,5,7,9,11,13,15,17,19,..., dimensions={0} | all-to-all | bytes 7864320 | tf_op jit(solution)/shard_map/all_to_all | solution.py:205
  297.3 5.4 %collective-permute-start.1 = (bf16[16,60,16,128]{3,2,1,0:T(8,128)(2,1)}, bf16[16,60,16,128]{3,2,1,0:T(8,128)(2,1)}, u32[]{:S(2)}, u32[]{:S(2)}) collective-permute-start(bf16[16,60,16,128]{3,2,1,0:T(8,128)(2,1)} %all_to_all.22.hidden_ref), channel_id=1, source_target_pairs={{0,1},{1,0},{2,3},{3,2},{4,5},{5,4},{6,7},{7,6},{8,9},{9,8},{10,11... | collective-permute-start | bytes 11796488 | tf_op jit(solution)/shard_map/ppermute | solution.py:281
  302.7 2.8 shard_map.116
  305.5 0.0 copy-start.2
  305.5 3.9 %collective-permute-done.1.hidden_ref = bf16[16,60,16,128]{3,2,1,0:T(8,128)(2,1)} collective-permute-done((bf16[16,60,16,128]{3,2,1,0:T(8,128)(2,1)}, bf16[16,60,16,128]{3,2,1,0:T(8,128)(2,1)}, u32[]{:S(2)}, u32[]{:S(2)}) %collective-permute-start.1) | collective-permute-done | bytes 3932192 | tf_op jit(solution)/shard_map/ppermute | solution.py:281
  309.4 2.8 shard_map.117
  312.2 1.5 copy-done
  313.7 0.7 pad_maximum_fusion.1
  314.4 6.4 %shard_map.118 = (bf16[32,48,128]{2,1,0:T(8,128)(2,1)}, bf16[32,48,128]{2,1,0:T(8,128)(2,1)}, bf16[32,48,128]{2,1,0:T(8,128)(2,1)}) custom-call(s32[32]{0:T(128)S(1)} %copy-done.2, s32[1]{0:T(128)} %bitcast.core_ref, bf16[32,144,256]{2,1,0:T(8,128)(2,1)S(1)} %get-tuple-element.20.mine_ref, bf16[32,144,256]{2,1,0:T(8,128)(2,1)} %copy-done, ...), custom_call_target="tpu_custom_call" | custom-call | flops 3221225472 | bytes 12582912 | tf_op jit(solution)/shard_map/pallas_call | solution.py:310
  (11 shorter events, 0.0 us)
Async XLA Ops:
  7.2 33.1 %copy-start.4 = (f32[512]{0:T(512)S(1)}, f32[512]{0:T(512)}, u32[]{:S(2)}) copy-start(f32[512]{0:T(512)} %param.10) | copy-start | bytes 6148
  7.2 33.2 %copy-start.3 = (bf16[512,128]{1,0:T(8,128)(2,1)S(1)}, bf16[512,128]{1,0:T(8,128)(2,1)}, u32[]{:S(2)}) copy-start(bf16[512,128]{1,0:T(8,128)(2,1)} %param.9) | copy-start | bytes 393220
  7.2 33.3 %copy-start.1 = (bf16[512,128]{1,0:T(8,128)(2,1)S(1)}, bf16[512,128]{1,0:T(8,128)(2,1)}, u32[]{:S(2)}) copy-start(bf16[512,128]{1,0:T(8,128)(2,1)} %rows_ref.3) | copy-start | bytes 393220
  10.3 144.8 %all-to-all-start = ((bf16[32,144,128]{2,1,0:T(8,128)(2,1)}), bf16[32,144,128]{2,1,0:T(8,128)(2,1)S(1)}, u32[]{:S(2)}, u32[]{:S(2)}) async-start(bf16[32,144,128]{2,1,0:T(8,128)(2,1)} %shard_map.111), calls=%async_computation | async-start | bytes 2359296 | tf_op jit(solution)/shard_map/all_to_all | solution.py:226
  39.6 274.8 %all-gather.2.cloned.1.call-start = ((), (), s32[]{:S(2)}) async-start(), calls=%async_computation.4 | async-start | bytes 8650752 | tf_op jit(solution)/shard_map/all_gather | solution.py:235
  155.9 6.8 %collective-permute-start = (bf16[256,4608]{1,0:T(8,128)(2,1)S(1)}, bf16[256,4608]{1,0:T(8,128)(2,1)S(1)}, u32[]{:S(2)}, u32[]{:S(2)}) collective-permute-start(bf16[256,4608]{1,0:T(8,128)(2,1)S(1)} %shard_map.112), channel_id=1, source_target_pairs={{0,1},{1,0},{2,3},{3,2},{4,5},{5,4},{6,7},{7,6},{8,9},{9,8},{10,11... | collective-permute-start | bytes 7077896 | tf_op jit(solution)/shard_map/ppermute | solution.py:249
  297.3 12.1 %collective-permute-start.1 = (bf16[16,60,16,128]{3,2,1,0:T(8,128)(2,1)}, bf16[16,60,16,128]{3,2,1,0:T(8,128)(2,1)}, u32[]{:S(2)}, u32[]{:S(2)}) collective-permute-start(bf16[16,60,16,128]{3,2,1,0:T(8,128)(2,1)} %all_to_all.22.hidden_ref), channel_id=1, source_target_pairs={{0,1},{1,0},{2,3},{3,2},{4,5},{5,4},{6,7},{7,6},{8,9},{9,8},{10,11... | collective-permute-start | bytes 11796488 | tf_op jit(solution)/shard_map/ppermute | solution.py:281
  305.5 8.9 %copy-start.2 = (s32[32]{0:T(128)S(1)}, s32[32]{0:T(128)}, u32[]{:S(2)}) copy-start(s32[32]{0:T(128)} %expert_ref.3) | copy-start | bytes 388
  312.2 1.5 copy-start
Sparse Core Ops, SparseCore 0:
  155.2 141.0 all-gather.1

commit v5 on v4

--- a/solution.py
+++ b/solution.py
@@ -10,6 +10,7 @@
 LANES = 128
 VMEM_LIMIT = 20 * 1024 * 1024
 LARGE_VMEM_LIMIT = 50 * 1024 * 1024
+TURNED_VMEM_LIMIT = 20 * 1024 * 1024
 GATHER_VMEM_LIMIT = 60 * 1024 * 1024
 
 
@@ -19,17 +20,28 @@
     )
 
 
-def gather_kernel(piece, expert_ref, gate_ref, up_ref, down_ref, out_ref, weights_ref, sems):
-    copies = [
-        pltpu.make_async_copy(weight_ref, weights_ref.at[m], sems.at[m])
+def gather_kernel(
+    piece, expert_ref, gate_ref, up_ref, down_ref, out_ref, weights_ref, chosen_ref, in_sems, out_sems
+):
+    arrivals = [
+        pltpu.make_async_copy(weight_ref, weights_ref.at[m], in_sems.at[m])
         for m, weight_ref in enumerate((gate_ref, up_ref, down_ref))
     ]
-    for copy in copies:
+    for copy in arrivals:
         copy.start()
-    for m, copy in enumerate(copies):
+    leavings = []
+    for m, copy in enumerate(arrivals):
         copy.wait()
         for group in range(out_ref.shape[0]):
-            out_ref[group, m * piece : (m + 1) * piece] = weights_ref[m, expert_ref[group]]
+            chosen_ref[m, group] = weights_ref[m, expert_ref[group]]
+        leavings.append(
+            pltpu.make_async_copy(
+                chosen_ref.at[m], out_ref.at[:, pl.ds(m * piece, piece)], out_sems.at[m]
+            )
+        )
+        leavings[m].start()
+    for copy in leavings:
+        copy.wait()
 
 
 def flat(weights_ref, m, piece):
@@ -112,7 +124,8 @@
         copies_ref[chip] = copies_ref[0]
 
 
-def turned_kernel(tail, piece, hidden_ref, weights_ref, turned_ref, rows_ref):
+def turned_kernel(tail, piece, core_ref, hidden_ref, weights_ref, *refs):
+    *first_ref, turned_ref, rows_ref = refs
     groups, _, half = turned_ref.shape
     per = LANES // tail
     for block in range(groups // per):
@@ -123,7 +136,7 @@
             turned_ref[group, LANES:] = rest[k * tail : (k + 1) * tail]
     first = groups + groups // per
     blocks = (hidden_ref.shape[1] - first) // 2
-    total = jnp.zeros(rows_ref.shape, jnp.float32)
+    total = jnp.zeros((half, rows_ref.shape[1]), jnp.float32)
     for m in range(2):
         weights = flat(weights_ref, m, piece)
         for k in range(blocks):
@@ -132,7 +145,13 @@
                 weights[k * LANES : (k + 1) * LANES],
                 preferred_element_type=jnp.float32,
             )
-    rows_ref[...] = total.astype(rows_ref.dtype)
+    total = total.astype(rows_ref.dtype)
+    if first_ref:
+        core = core_ref[0]
+        rows_ref[pl.ds(pl.multiple_of(core * half, half), half)] = first_ref[0][...]
+        rows_ref[pl.ds(pl.multiple_of((1 - core) * half, half), half)] = total
+    else:
+        rows_ref[...] = total
 
 
 def weight_kernel(
@@ -153,24 +172,28 @@
 ):
     groups = rows_ref.shape[0]
     per = groups // steps
-    sides = [
-        pltpu.make_async_copy(ref, turned_ref.at[i], sems.at[steps + i])
-        for i, ref in enumerate((mine_ref, other_ref))
-    ]
-    for copy in sides:
-        copy.start()
     copies = []
     for step in range(steps):
         cut = pl.ds(step * per, per)
-        copies.append(pltpu.make_async_copy(rows_ref.at[cut], held_ref.at[cut], sems.at[step]))
-        copies[step].start()
+        pairs = (
+            (mine_ref.at[cut], turned_ref.at[0, cut]),
+            (other_ref.at[cut], turned_ref.at[1, cut]),
+            (rows_ref.at[cut], held_ref.at[cut]),
+        )
+        copies.append(
+            [
+                pltpu.make_async_copy(source, target, sems.at[3 * step + i])
+                for i, (source, target) in enumerate(pairs)
+            ]
+        )
+        for copy in copies[step]:
+            copy.start()
     total_ref[...] = jnp.zeros_like(total_ref)
     core = core_ref[0]
-    for copy in sides:
-        copy.wait()
     for group in range(groups):
         if group % per == 0:
-            copies[group // per].wait()
+            for copy in copies[group // per]:
+                copy.wait()
         expert = expert_ref[group]
         term = jnp.dot(
             turned_ref[0, group], held_ref[group, core], preferred_element_type=jnp.float32
@@ -215,10 +238,12 @@
     outgoing = pl.pallas_call(
         functools.partial(gather_kernel, unit_piece),
         in_specs=[in_smem, in_place, in_place, in_place],
-        out_specs=in_vmem,
+        out_specs=in_place,
         out_shape=jax.ShapeDtypeStruct((groups, 3 * unit_piece, piece_width), jnp.bfloat16),
         scratch_shapes=[
             pltpu.VMEM((3, *gate_weight.shape), jnp.bfloat16),
+            pltpu.VMEM((3, groups, unit_piece, piece_width), jnp.bfloat16),
+            pltpu.SemaphoreType.DMA((3,)),
             pltpu.SemaphoreType.DMA((3,)),
         ],
         compiler_params=pltpu.CompilerParams(vmem_limit_bytes=GATHER_VMEM_LIMIT),
@@ -280,30 +305,25 @@
     hidden_mine = among_chips(copies)
     hidden_other = lax.ppermute(hidden_mine, "dp", partners)
 
-    def turned(hidden):
+    def turned(hidden, *first):
         return pl.pallas_call(
             functools.partial(turned_kernel, tail, unit_piece),
+            in_specs=[in_smem] + [in_vmem] * (2 + len(first)),
+            out_specs=(in_vmem, in_vmem),
             out_shape=(
                 jax.ShapeDtypeStruct((groups, 3 * unit_piece, half), jnp.bfloat16),
-                jax.ShapeDtypeStruct((half, piece_width), jnp.bfloat16),
+                jax.ShapeDtypeStruct((half * (1 + len(first)), piece_width), jnp.bfloat16),
             ),
-            compiler_params=roomy,
+            compiler_params=pltpu.CompilerParams(vmem_limit_bytes=TURNED_VMEM_LIMIT),
             cost_estimate=pl.CostEstimate(
                 flops=2 * row_count * units_all * piece_width,
                 bytes_accessed=7 * 1024 * 1024,
                 transcendentals=0,
             ),
-        )(hidden, fetched)
+        )(core_index, hidden, fetched, *first)
 
     turned_mine, grad_mine = turned(hidden_mine)
-    turned_other, grad_other = turned(hidden_other)
-    rows_grad = jnp.concatenate(
-        [
-            jnp.where(core == 0, grad_mine, grad_other),
-            jnp.where(core == 0, grad_other, grad_mine),
-        ],
-        axis=0,
-    )
+    turned_other, rows_grad = turned(hidden_other, grad_mine)
 
     rows_by_half = rows_all.reshape(groups, 2, half, 2 * piece_width)
     grad_shape = (experts_all, unit_piece, piece_width)
@@ -316,7 +336,7 @@
             pltpu.VMEM((2, *turned_mine.shape), jnp.bfloat16),
             pltpu.VMEM(rows_by_half.shape, jnp.bfloat16),
             pltpu.VMEM((experts_all, 3 * unit_piece, piece_width), jnp.float32),
-            pltpu.SemaphoreType.DMA((8 + 2,)),
+            pltpu.SemaphoreType.DMA((3 * 8,)),
         ],
         compiler_params=pltpu.CompilerParams(vmem_limit_bytes=LARGE_VMEM_LIMIT),
         cost_estimate=pl.CostEstimate(

time: 328 us -> 326 us (level)
  Pallas kernels: 17.8 us -> 13.9 us
    pallas_call x2, Pallas kernels: 5.6 us -> 1.94 us  [turned(): pl.pallas_call(functools.partial(turned_kernel, tail, unit_piece), in_spe...]
  transfers between devices with their start and end apart: 4 -> 4, of which waited for: 3 -> 3; matrix products, arithmetic and copies ran while one was open for 0% -> 0% of each run, Pallas kernels for 3% -> 1%
where the time goes in v5:
time: 326 us
  blocking collectives  134 us (41%)
  waiting for transfers between devices  124 us (38%)
  starting transfers between devices  37.4 us (11%)
  between operations  14.8 us (5%)
  Pallas kernels  13.9 us (4%)
    all_to_all x1, waiting for transfers between devices, shards(): lax.all_to_all(outgoing, 'expert', split_axis=0, concat_axis=0, tiled=True)  114 us
    all_to_all x2, blocking collectives, among_chips(): lax.all_to_all(blocks, 'dp', split_axis=0, concat_axis=0, tiled=True, axi...  88.1 us
    all_to_all x1, blocking collectives, shards(): lax.all_to_all(pieces, 'expert', split_axis=0, concat_axis=0, tiled=True)  45.7 us
    all_to_all x1, starting transfers between devices, shards(): lax.all_to_all(outgoing, 'expert', split_axis=0, concat_axis=0, tiled=True)  29.3 us
  transfers between devices with their start and end apart: 4, of which 3 were waited for; matrix products, arithmetic and copies ran while one was open for 0% of the time, Pallas kernels for 1%

profile of v5, /device:TPU:1, one launch (start us, length us, event | category | flops | bytes accessed | tf_op | source)
XLA Modules:
  0.0 325.9 jit_solution(14505547405969547293)
XLA Ops:
  7.2 2.9 shard_map.111
  10.2 29.3 %all-to-all-start = ((bf16[32,144,128]{2,1,0:T(8,128)(2,1)}), bf16[32,144,128]{2,1,0:T(8,128)(2,1)S(1)}, u32[]{:S(2)}, u32[]{:S(2)}) async-start(bf16[32,144,128]{2,1,0:T(8,128)(2,1)} %shard_map.111), calls=%async_computation | async-start | bytes 2359296 | tf_op jit(solution)/shard_map/all_to_all | solution.py:251
  39.5 0.0 all-gather.2.cloned.1.call-start
  40.1 0.0 copy-done.4
  40.2 0.1 multiply_convert_fusion.scaled_ref
  40.3 0.0 copy-done.1
  40.3 0.7 pad_maximum_fusion
  41.1 113.9 %all-to-all-done.weights_ref = bf16[32,144,128]{2,1,0:T(8,128)(2,1)S(1)} async-done(((bf16[32,144,128]{2,1,0:T(8,128)(2,1)}), bf16[32,144,128]{2,1,0:T(8,128)(2,1)S(1)}, u32[]{:S(2)}, u32[]{:S(2)}) %all-to-all-start) | async-done | bytes 1179680 | tf_op jit(solution)/shard_map/all_to_all | solution.py:251
  154.9 0.0 all-gather.2.cloned.1.call-update
  155.0 0.8 shard_map.112
  155.7 2.6 collective-permute-start
  158.4 4.1 %collective-permute-done.got_ref = bf16[256,4608]{1,0:T(8,128)(2,1)S(1)} collective-permute-done((bf16[256,4608]{1,0:T(8,128)(2,1)S(1)}, bf16[256,4608]{1,0:T(8,128)(2,1)S(1)}, u32[]{:S(2)}, u32[]{:S(2)}) %collective-permute-start) | collective-permute-done | bytes 2359328 | tf_op jit(solution)/shard_map/ppermute | solution.py:274
  162.5 0.8 shard_map.113
  163.3 37.2 %all_to_all.20.parts_ref = bf16[16,16,4608]{2,1,0:T(8,128)(2,1)S(1)} all-to-all(bf16[16,16,4608]{2,1,0:T(8,128)(2,1)S(1)} %bitcast.5), channel_id=1, replica_groups={{0,2,4,6,8,10,12,14,16,18,20,22,24,26,28,30},{1,3,5,7,9,11,13,15,17,19,..., dimensions={0} | all-to-all | bytes 4718592 | tf_op jit(solution)/shard_map/all_to_all | solution.py:228
  200.5 0.5 shard_map.114
  201.0 45.7 %all_to_all.21.pieces_ref = bf16[32,8,384]{2,1,0:T(8,128)(2,1)S(1)} all-to-all(bf16[32,8,384]{2,1,0:T(8,128)(2,1)S(1)} %get-tuple-element.16), channel_id=1, replica_groups=mesh['expert'=32,'dp'=32] {'expert'}, dimensions={0} | all-to-all | bytes 393216 | tf_op jit(solution)/shard_map/all_to_all | solution.py:296
  246.7 0.6 shard_map.115
  247.3 50.8 %all_to_all.22.hidden_ref = bf16[16,60,16,128]{3,2,1,0:T(8,128)(2,1)S(1)} all-to-all(bf16[16,60,16,128]{3,2,1,0:T(8,128)(2,1)S(1)} %shard_map.115), channel_id=1, replica_groups={{0,2,4,6,8,10,12,14,16,18,20,22,24,26,28,30},{1,3,5,7,9,11,13,15,17,19,..., dimensions={0} | all-to-all | bytes 7864320 | tf_op jit(solution)/shard_map/all_to_all | solution.py:228
  298.2 5.4 %collective-permute-start.1 = (bf16[16,60,16,128]{3,2,1,0:T(8,128)(2,1)S(1)}, bf16[16,60,16,128]{3,2,1,0:T(8,128)(2,1)S(1)}, u32[]{:S(2)}, u32[]{:S(2)}) collective-permute-start(bf16[16,60,16,128]{3,2,1,0:T(8,128)(2,1)S(1)} %all_to_all.22.hidden_ref), channel_id=1, source_target_pairs={{0,1},{1,0},{2,3},{3,2},{4,5},{5,4},{6,7},{7,6},{8,9},{9,8},{10,11... | collective-permute-start | bytes 11796488 | tf_op jit(solution)/shard_map/ppermute | solution.py:306
  303.6 0.7 shard_map.116
  304.3 5.7 %collective-permute-done.1.hidden_ref = bf16[16,60,16,128]{3,2,1,0:T(8,128)(2,1)S(1)} collective-permute-done((bf16[16,60,16,128]{3,2,1,0:T(8,128)(2,1)S(1)}, bf16[16,60,16,128]{3,2,1,0:T(8,128)(2,1)S(1)}, u32[]{:S(2)}, u32[]{:S(2)}) %collective-permute-start.1) | collective-permute-done | bytes 3932192 | tf_op jit(solution)/shard_map/ppermute | solution.py:306
  310.0 1.2 shard_map.117
  311.2 1.5 copy-done
  312.7 6.4 %shard_map.118 = (bf16[32,48,128]{2,1,0:T(8,128)(2,1)}, bf16[32,48,128]{2,1,0:T(8,128)(2,1)}, bf16[32,48,128]{2,1,0:T(8,128)(2,1)}) custom-call(s32[32]{0:T(128)S(1)} %copy-done.2, s32[1]{0:T(128)} %bitcast.core_ref, bf16[32,144,256]{2,1,0:T(8,128)(2,1)S(1)} %get-tuple-element.20.mine_ref, bf16[32,144,256]{2,1,0:T(8,128)(2,1)} %copy-done, ...), custom_call_target="tpu_custom_call" | custom-call | flops 3221225472 | bytes 12582912 | tf_op jit(solution)/shard_map/pallas_call | solution.py:330
  (9 shorter events, 0.0 us)
Async XLA Ops:
  7.2 33.0 %copy-start.4 = (f32[512]{0:T(512)S(1)}, f32[512]{0:T(512)}, u32[]{:S(2)}) copy-start(f32[512]{0:T(512)} %param.10) | copy-start | bytes 6148
  7.2 33.0 %copy-start.3 = (bf16[512,128]{1,0:T(8,128)(2,1)S(1)}, bf16[512,128]{1,0:T(8,128)(2,1)}, u32[]{:S(2)}) copy-start(bf16[512,128]{1,0:T(8,128)(2,1)} %param.9) | copy-start | bytes 393220
  7.2 33.1 %copy-start.1 = (bf16[512,128]{1,0:T(8,128)(2,1)S(1)}, bf16[512,128]{1,0:T(8,128)(2,1)}, u32[]{:S(2)}) copy-start(bf16[512,128]{1,0:T(8,128)(2,1)} %rows_ref.3) | copy-start | bytes 393220
  10.2 144.8 %all-to-all-start = ((bf16[32,144,128]{2,1,0:T(8,128)(2,1)}), bf16[32,144,128]{2,1,0:T(8,128)(2,1)S(1)}, u32[]{:S(2)}, u32[]{:S(2)}) async-start(bf16[32,144,128]{2,1,0:T(8,128)(2,1)} %shard_map.111), calls=%async_computation | async-start | bytes 2359296 | tf_op jit(solution)/shard_map/all_to_all | solution.py:251
  39.5 273.3 %all-gather.2.cloned.1.call-start = ((), (), s32[]{:S(2)}) async-start(), calls=%async_computation.4 | async-start | bytes 8650752 | tf_op jit(solution)/shard_map/all_gather | solution.py:260
  155.7 6.8 %collective-permute-start = (bf16[256,4608]{1,0:T(8,128)(2,1)S(1)}, bf16[256,4608]{1,0:T(8,128)(2,1)S(1)}, u32[]{:S(2)}, u32[]{:S(2)}) collective-permute-start(bf16[256,4608]{1,0:T(8,128)(2,1)S(1)} %shard_map.112), channel_id=1, source_target_pairs={{0,1},{1,0},{2,3},{3,2},{4,5},{5,4},{6,7},{7,6},{8,9},{9,8},{10,11... | collective-permute-start | bytes 7077896 | tf_op jit(solution)/shard_map/ppermute | solution.py:274
  298.2 11.8 %collective-permute-start.1 = (bf16[16,60,16,128]{3,2,1,0:T(8,128)(2,1)S(1)}, bf16[16,60,16,128]{3,2,1,0:T(8,128)(2,1)S(1)}, u32[]{:S(2)}, u32[]{:S(2)}) collective-permute-start(bf16[16,60,16,128]{3,2,1,0:T(8,128)(2,1)S(1)} %all_to_all.22.hidden_ref), channel_id=1, source_target_pairs={{0,1},{1,0},{2,3},{3,2},{4,5},{5,4},{6,7},{7,6},{8,9},{9,8},{10,11... | collective-permute-start | bytes 11796488 | tf_op jit(solution)/shard_map/ppermute | solution.py:306
  310.0 2.7 copy-start.2
  311.2 1.5 copy-start
Sparse Core Ops, SparseCore 0:
  155.1 140.6 all-gather.1

commit v6 on v5

--- a/solution.py
+++ b/solution.py
@@ -170,37 +170,33 @@
     total_ref,
     sems,
 ):
-    groups = rows_ref.shape[0]
+    groups, _, half, _ = rows_ref.shape
     per = groups // steps
+    core = core_ref[0]
     copies = []
     for step in range(steps):
         cut = pl.ds(step * per, per)
         pairs = (
-            (mine_ref.at[cut], turned_ref.at[0, cut]),
-            (other_ref.at[cut], turned_ref.at[1, cut]),
-            (rows_ref.at[cut], held_ref.at[cut]),
+            (mine_ref.at[cut], turned_ref.at[cut, :, pl.ds(0, half)]),
+            (other_ref.at[cut], turned_ref.at[cut, :, pl.ds(half, half)]),
+            (rows_ref.at[cut, core], held_ref.at[cut, pl.ds(0, half)]),
+            (rows_ref.at[cut, 1 - core], held_ref.at[cut, pl.ds(half, half)]),
         )
         copies.append(
             [
-                pltpu.make_async_copy(source, target, sems.at[3 * step + i])
+                pltpu.make_async_copy(source, target, sems.at[4 * step + i])
                 for i, (source, target) in enumerate(pairs)
             ]
         )
         for copy in copies[step]:
             copy.start()
     total_ref[...] = jnp.zeros_like(total_ref)
-    core = core_ref[0]
     for group in range(groups):
         if group % per == 0:
             for copy in copies[group // per]:
                 copy.wait()
         expert = expert_ref[group]
-        term = jnp.dot(
-            turned_ref[0, group], held_ref[group, core], preferred_element_type=jnp.float32
-        )
-        term += jnp.dot(
-            turned_ref[1, group], held_ref[group, 1 - core], preferred_element_type=jnp.float32
-        )
+        term = jnp.dot(turned_ref[group], held_ref[group], preferred_element_type=jnp.float32)
         total_ref[expert, : 2 * piece] += term[: 2 * piece, :LANES]
         total_ref[expert, 2 * piece :] += term[2 * piece :, LANES:]
     for m, out_ref in enumerate((gate_ref, up_ref, down_ref)):
@@ -333,10 +329,10 @@
         out_specs=(in_vmem,) * 3,
         out_shape=tuple(jax.ShapeDtypeStruct(grad_shape, jnp.bfloat16) for _ in range(3)),
         scratch_shapes=[
-            pltpu.VMEM((2, *turned_mine.shape), jnp.bfloat16),
-            pltpu.VMEM(rows_by_half.shape, jnp.bfloat16),
+            pltpu.VMEM((groups, 3 * unit_piece, row_count), jnp.bfloat16),
+            pltpu.VMEM((groups, row_count, 2 * piece_width), jnp.bfloat16),
             pltpu.VMEM((experts_all, 3 * unit_piece, piece_width), jnp.float32),
-            pltpu.SemaphoreType.DMA((3 * 8,)),
+            pltpu.SemaphoreType.DMA((4 * 8,)),
         ],
         compiler_params=pltpu.CompilerParams(vmem_limit_bytes=LARGE_VMEM_LIMIT),
         cost_estimate=pl.CostEstimate(

time: 326 us -> 326 us (level)
  no operation moved by 1% of the time
where the time goes in v6:
time: 326 us
  blocking collectives  134 us (41%)
  waiting for transfers between devices  124 us (38%)
  starting transfers between devices  37.4 us (11%)
  between operations  14.8 us (5%)
  Pallas kernels  13.8 us (4%)
    all_to_all x1, waiting for transfers between devices, shards(): lax.all_to_all(outgoing, 'expert', split_axis=0, concat_axis=0, tiled=True)  114 us
    all_to_all x2, blocking collectives, among_chips(): lax.all_to_all(blocks, 'dp', split_axis=0, concat_axis=0, tiled=True, axi...  88.2 us
    all_to_all x1, blocking collectives, shards(): lax.all_to_all(pieces, 'expert', split_axis=0, concat_axis=0, tiled=True)  45.5 us
    all_to_all x1, starting transfers between devices, shards(): lax.all_to_all(outgoing, 'expert', split_axis=0, concat_axis=0, tiled=True)  29.3 us
  transfers between devices with their start and end apart: 4, of which 3 were waited for; matrix products, arithmetic and copies ran while one was open for 0% of the time, Pallas kernels for 1%

profile of v6, /device:TPU:1, one launch (start us, length us, event | category | flops | bytes accessed | tf_op | source)
XLA Modules:
  0.0 325.9 jit_solution(12031818024816266277)
XLA Ops:
  7.2 0.0 copy-start.4
  7.2 0.0 copy-start.3
  7.2 2.9 shard_map.111
  10.2 29.3 %all-to-all-start = ((bf16[32,144,128]{2,1,0:T(8,128)(2,1)}), bf16[32,144,128]{2,1,0:T(8,128)(2,1)S(1)}, u32[]{:S(2)}, u32[]{:S(2)}) async-start(bf16[32,144,128]{2,1,0:T(8,128)(2,1)} %shard_map.111), calls=%async_computation | async-start | bytes 2359296 | tf_op jit(solution)/shard_map/all_to_all | solution.py:247
  39.5 0.0 all-gather.2.cloned.1.call-start
  40.2 0.1 multiply_convert_fusion.scaled_ref
  40.3 0.7 pad_maximum_fusion
  41.1 113.9 %all-to-all-done.weights_ref = bf16[32,144,128]{2,1,0:T(8,128)(2,1)S(1)} async-done(((bf16[32,144,128]{2,1,0:T(8,128)(2,1)}), bf16[32,144,128]{2,1,0:T(8,128)(2,1)S(1)}, u32[]{:S(2)}, u32[]{:S(2)}) %all-to-all-start) | async-done | bytes 1179680 | tf_op jit(solution)/shard_map/all_to_all | solution.py:247
  154.9 0.0 all-gather.2.cloned.1.call-update
  155.0 0.8 shard_map.112
  155.7 2.6 collective-permute-start
  158.4 4.1 %collective-permute-done.got_ref = bf16[256,4608]{1,0:T(8,128)(2,1)S(1)} collective-permute-done((bf16[256,4608]{1,0:T(8,128)(2,1)S(1)}, bf16[256,4608]{1,0:T(8,128)(2,1)S(1)}, u32[]{:S(2)}, u32[]{:S(2)}) %collective-permute-start) | collective-permute-done | bytes 2359328 | tf_op jit(solution)/shard_map/ppermute | solution.py:270
  162.5 0.8 shard_map.113
  163.3 37.2 %all_to_all.20.parts_ref = bf16[16,16,4608]{2,1,0:T(8,128)(2,1)S(1)} all-to-all(bf16[16,16,4608]{2,1,0:T(8,128)(2,1)S(1)} %bitcast.5), channel_id=1, replica_groups={{0,2,4,6,8,10,12,14,16,18,20,22,24,26,28,30},{1,3,5,7,9,11,13,15,17,19,..., dimensions={0} | all-to-all | bytes 4718592 | tf_op jit(solution)/shard_map/all_to_all | solution.py:224
  200.5 0.5 shard_map.114
  201.0 45.5 %all_to_all.21.pieces_ref = bf16[32,8,384]{2,1,0:T(8,128)(2,1)S(1)} all-to-all(bf16[32,8,384]{2,1,0:T(8,128)(2,1)S(1)} %get-tuple-element.16), channel_id=1, replica_groups=mesh['expert'=32,'dp'=32] {'expert'}, dimensions={0} | all-to-all | bytes 393216 | tf_op jit(solution)/shard_map/all_to_all | solution.py:292
  246.6 0.6 shard_map.115
  247.2 51.0 %all_to_all.22.hidden_ref = bf16[16,60,16,128]{3,2,1,0:T(8,128)(2,1)S(1)} all-to-all(bf16[16,60,16,128]{3,2,1,0:T(8,128)(2,1)S(1)} %shard_map.115), channel_id=1, replica_groups={{0,2,4,6,8,10,12,14,16,18,20,22,24,26,28,30},{1,3,5,7,9,11,13,15,17,19,..., dimensions={0} | all-to-all | bytes 7864320 | tf_op jit(solution)/shard_map/all_to_all | solution.py:224
  298.2 5.4 %collective-permute-start.1 = (bf16[16,60,16,128]{3,2,1,0:T(8,128)(2,1)S(1)}, bf16[16,60,16,128]{3,2,1,0:T(8,128)(2,1)S(1)}, u32[]{:S(2)}, u32[]{:S(2)}) collective-permute-start(bf16[16,60,16,128]{3,2,1,0:T(8,128)(2,1)S(1)} %all_to_all.22.hidden_ref), channel_id=1, source_target_pairs={{0,1},{1,0},{2,3},{3,2},{4,5},{5,4},{6,7},{7,6},{8,9},{9,8},{10,11... | collective-permute-start | bytes 11796488 | tf_op jit(solution)/shard_map/ppermute | solution.py:302
  303.6 0.7 shard_map.116
  304.3 5.7 %collective-permute-done.1.hidden_ref = bf16[16,60,16,128]{3,2,1,0:T(8,128)(2,1)S(1)} collective-permute-done((bf16[16,60,16,128]{3,2,1,0:T(8,128)(2,1)S(1)}, bf16[16,60,16,128]{3,2,1,0:T(8,128)(2,1)S(1)}, u32[]{:S(2)}, u32[]{:S(2)}) %collective-permute-start.1) | collective-permute-done | bytes 3932192 | tf_op jit(solution)/shard_map/ppermute | solution.py:302
  310.0 1.2 shard_map.117
  311.3 1.5 copy-done
  312.7 6.3 %shard_map.118 = (bf16[32,48,128]{2,1,0:T(8,128)(2,1)}, bf16[32,48,128]{2,1,0:T(8,128)(2,1)}, bf16[32,48,128]{2,1,0:T(8,128)(2,1)}) custom-call(s32[32]{0:T(128)S(1)} %copy-done.2, s32[1]{0:T(128)} %bitcast.core_ref, bf16[32,144,256]{2,1,0:T(8,128)(2,1)S(1)} %get-tuple-element.20.mine_ref, bf16[32,144,256]{2,1,0:T(8,128)(2,1)} %copy-done, ...), custom_call_target="tpu_custom_call" | custom-call | flops 3221225472 | bytes 12582912 | tf_op jit(solution)/shard_map/pallas_call | solution.py:326
  (9 shorter events, 0.0 us)
Async XLA Ops:
  7.2 33.0 %copy-start.4 = (f32[512]{0:T(512)S(1)}, f32[512]{0:T(512)}, u32[]{:S(2)}) copy-start(f32[512]{0:T(512)} %param.10) | copy-start | bytes 6148
  7.2 33.0 %copy-start.3 = (bf16[512,128]{1,0:T(8,128)(2,1)S(1)}, bf16[512,128]{1,0:T(8,128)(2,1)}, u32[]{:S(2)}) copy-start(bf16[512,128]{1,0:T(8,128)(2,1)} %param.9) | copy-start | bytes 393220
  7.2 33.1 %copy-start.1 = (bf16[512,128]{1,0:T(8,128)(2,1)S(1)}, bf16[512,128]{1,0:T(8,128)(2,1)}, u32[]{:S(2)}) copy-start(bf16[512,128]{1,0:T(8,128)(2,1)} %rows_ref.3) | copy-start | bytes 393220
  10.2 144.8 %all-to-all-start = ((bf16[32,144,128]{2,1,0:T(8,128)(2,1)}), bf16[32,144,128]{2,1,0:T(8,128)(2,1)S(1)}, u32[]{:S(2)}, u32[]{:S(2)}) async-start(bf16[32,144,128]{2,1,0:T(8,128)(2,1)} %shard_map.111), calls=%async_computation | async-start | bytes 2359296 | tf_op jit(solution)/shard_map/all_to_all | solution.py:247
  39.5 273.3 %all-gather.2.cloned.1.call-start = ((), (), s32[]{:S(2)}) async-start(), calls=%async_computation.4 | async-start | bytes 8650752 | tf_op jit(solution)/shard_map/all_gather | solution.py:256
  155.7 6.8 %collective-permute-start = (bf16[256,4608]{1,0:T(8,128)(2,1)S(1)}, bf16[256,4608]{1,0:T(8,128)(2,1)S(1)}, u32[]{:S(2)}, u32[]{:S(2)}) collective-permute-start(bf16[256,4608]{1,0:T(8,128)(2,1)S(1)} %shard_map.112), channel_id=1, source_target_pairs={{0,1},{1,0},{2,3},{3,2},{4,5},{5,4},{6,7},{7,6},{8,9},{9,8},{10,11... | collective-permute-start | bytes 7077896 | tf_op jit(solution)/shard_map/ppermute | solution.py:270
  298.2 11.8 %collective-permute-start.1 = (bf16[16,60,16,128]{3,2,1,0:T(8,128)(2,1)S(1)}, bf16[16,60,16,128]{3,2,1,0:T(8,128)(2,1)S(1)}, u32[]{:S(2)}, u32[]{:S(2)}) collective-permute-start(bf16[16,60,16,128]{3,2,1,0:T(8,128)(2,1)S(1)} %all_to_all.22.hidden_ref), channel_id=1, source_target_pairs={{0,1},{1,0},{2,3},{3,2},{4,5},{5,4},{6,7},{7,6},{8,9},{9,8},{10,11... | collective-permute-start | bytes 11796488 | tf_op jit(solution)/shard_map/ppermute | solution.py:302
  310.0 2.7 copy-start.2
  311.3 1.5 copy-start
Sparse Core Ops, SparseCore 0:
  155.1 141.0 all-gather.1
